TPU v7x, 32 devices: a whole 2x2x4 slice. The times are simulated.
32 devices in a mesh: section: 4 (over y, x), dp: 4 (over z), mp: 2 (over core).
Axes of the slice: x: 2, y: 2, z: 4, core: 2. Of those that a mesh axis runs over, the one named last changes fastest.
Arguments:
- hidden_in: bfloat16 [8, 512, 768], P('dp', 'mp'), may hold values from -6 to 6
- segments: int32 [8, 512], P('dp'), may hold values from 0 to 5, never falling along the last dimension, each value on 1 to 256 neighbouring positions
- partners: int32 [8, 6], P('dp'), may hold values from 0 to 5, as said below
- queue: bfloat16 [16384, 768], P(('section', 'dp', 'mp')), may hold values from -6 to 6
- first_weight: bfloat16 [2, 4, 768, 4, 768], P(None, 'section', None, None, 'mp')
- second_weight: bfloat16 [2, 4, 2, 768, 768], P(None, 'section', None, 'mp'), may hold values from -0.109375 to 0.109375
- out_bias: float32 [2, 4, 768], P(None, 'section'), may hold values from -3 to 3
- ln_gain: float32 [2, 4, 768], P(None, 'section'), may hold values from 0.5 to 1.5
- ln_bias: float32 [2, 4, 768], P(None, 'section'), may hold values from -3 to 3
Outputs:
- loss: float32 [], replicated
- grad_input: bfloat16 [8, 512, 768], P('dp', 'mp', 'section')
- grad_first: float32 [4, 768, 4, 768], P('section', None, None, 'mp')
- grad_second: float32 [4, 2, 768, 768], P('section', None, 'mp')
- grad_out_bias: float32 [4, 768], P('section')
- grad_gain: float32 [4, 768], P('section')
- grad_ln_bias: float32 [4, 768], P('section')
Inputs may be any that keep to these rules, and one draw needn't show every extreme that they name: In each row the crops form pairs: partners[r, c] differs from c, and partners[r, partners[r, c]] = c.
All inputs are finite; a program needn't handle non-finite values.
Results may differ from a plain program's by a relative error of at most 0.025.
Values may be sent and summed in bfloat16 or wider, within the bound.
A program may use at most 256 MiB of HBM per device.

v0:
```python
import jax
import jax.numpy as jnp
from jax import lax
from jax.sharding import PartitionSpec as P

HD = 64
MICRO = 2


inv_tau = 20.0
layer_eps = 1e-12
unit_eps = 1e-06
neg_fill = -1e30


def as_sent(shard):

    def short(part):
        return part.astype(jnp.bfloat16) if part.dtype == jnp.float32 else part

    return jax.tree.map(short, shard)


def shifted(shard, axis, by):
    devices = lax.axis_size(axis)
    pairs = [(i, i + by) for i in range(devices) if 0 <= i + by < devices]
    return lax.ppermute(shard, axis, pairs)


def spread_2(value, axis, source):
    kept = jnp.where(lax.axis_index(axis) == source, value, 0).astype(value.dtype)
    return lax.psum(kept, axis)


def layer_norm(residual, norm_gain, norm_shift):
    centre = residual - jnp.mean(residual, axis=-1, keepdims=True)
    spread = jnp.mean(centre * centre, axis=-1, keepdims=True)
    return centre * lax.rsqrt(spread + layer_eps) * norm_gain + norm_shift


def unit_rows(vectors):
    return vectors * lax.rsqrt(jnp.sum(vectors * vectors, axis=-1, keepdims=True) + unit_eps)


def gelu_exact(values):
    return jax.nn.gelu(values, approximate=False)


def take_own(array_rows, start_row, own_count):
    return lax.dynamic_slice_in_dim(array_rows, start_row, own_count, 0)


def head_core(queries, key_rows, value_rows, same_crop):
    score_scale = HD ** (-0.5)
    scores = (
        jnp.einsum("qe,ke->qk", queries, key_rows, preferred_element_type=jnp.float32) * score_scale
    )
    scores = jnp.where(same_crop, scores, neg_fill)
    row_max = jnp.max(scores, axis=-1, keepdims=True)
    weights = jnp.exp(scores - row_max)
    attn_prob = weights / jnp.sum(weights, axis=-1, keepdims=True)
    prob_low = attn_prob.astype(jnp.bfloat16)
    mixed_out = jnp.dot(prob_low, value_rows, preferred_element_type=jnp.float32).astype(
        jnp.bfloat16
    )
    return (attn_prob, prob_low, mixed_out)


def attend_setup(hidden, segment, w_first):
    head_count = w_first.shape[2] // HD
    proj_qkv = w_first[:, :3].reshape(w_first.shape[0], 3, head_count, HD)
    proj_out = w_first[:, 3].reshape(w_first.shape[0], head_count, HD)
    qkv_low = jnp.einsum(
        "sd,djhe->jhse", hidden, proj_qkv, preferred_element_type=jnp.float32
    ).astype(jnp.bfloat16)
    same_crop = segment[:, None] == segment[None, :]
    return (head_count, proj_qkv, proj_out, qkv_low, same_crop)


def attend_row(hidden, segment, w_first):
    head_count, proj_qkv, proj_out, qkv_low, same_crop = attend_setup(hidden, segment, w_first)

    def one_head(head_index):
        picked = lax.dynamic_index_in_dim(qkv_low, head_index, 1, keepdims=False)
        return head_core(picked[0], picked[1], picked[2], same_crop)[2]

    mixed_out = lax.map(one_head, jnp.arange(head_count))
    return jnp.einsum("hse,dhe->sd", mixed_out, proj_out, preferred_element_type=jnp.float32)


def attend_row_grad(hidden, segment, w_first, branch_low):
    head_count, proj_qkv, proj_out, qkv_low, same_crop = attend_setup(hidden, segment, w_first)
    score_scale = HD ** (-0.5)

    def one_head(head_index):
        picked = lax.dynamic_index_in_dim(qkv_low, head_index, 1, keepdims=False)
        queries, key_rows, value_rows = (picked[0], picked[1], picked[2])
        attn_prob, prob_low, mixed_out = head_core(queries, key_rows, value_rows, same_crop)
        out_slice = lax.dynamic_index_in_dim(proj_out, head_index, 1, keepdims=False)
        grad_out_w = jnp.einsum(
            "sd,se->de", branch_low, mixed_out, preferred_element_type=jnp.float32
        )
        grad_mixed = jnp.dot(branch_low, out_slice, preferred_element_type=jnp.float32).astype(
            jnp.bfloat16
        )
        grad_prob = jnp.einsum(
            "qe,ke->qk", grad_mixed, value_rows, preferred_element_type=jnp.float32
        )
        grad_values = jnp.einsum(
            "qk,qe->ke", prob_low, grad_mixed, preferred_element_type=jnp.float32
        )
        grad_scores = attn_prob * (
            grad_prob - jnp.sum(attn_prob * grad_prob, axis=-1, keepdims=True)
        )
        grad_scores = grad_scores.astype(jnp.bfloat16)
        grad_queries = (
            jnp.dot(grad_scores, key_rows, preferred_element_type=jnp.float32) * score_scale
        )
        grad_keys = (
            jnp.einsum("qk,qe->ke", grad_scores, queries, preferred_element_type=jnp.float32)
            * score_scale
        )
        grad_stack = jnp.stack([grad_queries, grad_keys, grad_values]).astype(jnp.bfloat16)
        return (grad_stack, grad_out_w)

    grad_qkv, grad_out_w = lax.map(one_head, jnp.arange(head_count))
    model_width = hidden.shape[1]
    grad_proj = jnp.einsum("sd,hjse->djhe", hidden, grad_qkv, preferred_element_type=jnp.float32)
    grad_hidden = jnp.einsum(
        "hjse,djhe->sd", grad_qkv, proj_qkv, preferred_element_type=jnp.float32
    )
    grad_out_cols = jnp.swapaxes(grad_out_w, 0, 1).reshape(model_width, 1, -1)
    grad_first = jnp.concatenate([grad_proj.reshape(model_width, 3, -1), grad_out_cols], axis=1)
    return (grad_hidden, grad_first)


def feed_parts(hidden, w_first):
    up_proj = jnp.einsum("rsd,djc->rsjc", hidden, w_first, preferred_element_type=jnp.float32)
    return (up_proj, gelu_exact(up_proj).astype(jnp.bfloat16))


def feed_partial(hidden, w_first, w_down):
    up_proj, activated = feed_parts(hidden, w_first)
    return jnp.einsum("rsjc,jcd->rsd", activated, w_down, preferred_element_type=jnp.float32)


def feed_grad(hidden, w_first, w_down, branch_low):
    up_proj, activated = feed_parts(hidden, w_first)
    grad_down = jnp.einsum(
        "rsjc,rsd->jcd", activated, branch_low, preferred_element_type=jnp.float32
    )
    grad_act = jnp.einsum("rsd,jcd->rsjc", branch_low, w_down, preferred_element_type=jnp.float32)
    grad_up = jax.vjp(gelu_exact, up_proj)[1](grad_act)[0].astype(jnp.bfloat16)
    grad_first = jnp.einsum("rsd,rsjc->djc", hidden, grad_up, preferred_element_type=jnp.float32)
    grad_hidden = jnp.einsum("rsjc,djc->rsd", grad_up, w_first, preferred_element_type=jnp.float32)
    return (grad_hidden, grad_first, grad_down)


def branch_partial(branch_mode, whole_rows, segment, w_first, w_down):

    def spare_side(operands):
        return jnp.zeros(operands[0].shape, jnp.float32)

    def attention_side(operands):
        hidden, segment_rows, first_w, down_w = operands
        return lax.map(
            lambda row_pair: attend_row(row_pair[0], row_pair[1], first_w), (hidden, segment_rows)
        )

    def feed_side(operands):
        hidden, segment_rows, first_w, down_w = operands
        return feed_partial(hidden, first_w, down_w)

    return lax.switch(
        branch_mode, [spare_side, attention_side, feed_side], (whole_rows, segment, w_first, w_down)
    )


def branch_grad(branch_mode, whole_rows, segment, w_first, w_down, branch_low):

    def spare_side(operands):
        return (
            jnp.zeros(operands[0].shape, jnp.float32),
            jnp.zeros(operands[2].shape, jnp.float32),
            jnp.zeros(operands[3].shape, jnp.float32),
        )

    def attention_side(operands):
        hidden, segment_rows, first_w, down_w, grad_rows = operands
        grad_hidden, grad_first = lax.map(
            lambda row_pack: attend_row_grad(row_pack[0], row_pack[1], first_w, row_pack[2]),
            (hidden, segment_rows, grad_rows),
        )
        return (grad_hidden, jnp.sum(grad_first, axis=0), jnp.zeros(down_w.shape, jnp.float32))

    def feed_side(operands):
        hidden, segment_rows, first_w, down_w, grad_rows = operands
        return feed_grad(hidden, first_w, down_w, grad_rows)

    return lax.switch(
        branch_mode,
        [spare_side, attention_side, feed_side],
        (whole_rows, segment, w_first, w_down, branch_low),
    )


def widen_rows(local_rows):
    return lax.all_gather(local_rows, "mp", axis=1, tiled=True)


def narrow(partial_value):
    return jax.tree.map(
        lambda part: part.astype(jnp.float32),
        lax.psum_scatter(as_sent(partial_value), "mp", scatter_dimension=1, tiled=True),
    )


def section_forward(branch_mode, hidden_local, segment, weights):
    w_first, w_down, out_bias, norm_gain, norm_shift = weights
    combined = narrow(
        branch_partial(branch_mode, widen_rows(hidden_local), segment, w_first, w_down)
    )
    residual = hidden_local.astype(jnp.float32) + combined + out_bias
    return (layer_norm(residual, norm_gain, norm_shift), combined)


def section_backward(branch_mode, hidden_local, segment, weights, grad_out, kept_sum):
    w_first, w_down, out_bias, norm_gain, norm_shift = weights
    whole_rows = widen_rows(hidden_local)
    residual = hidden_local.astype(jnp.float32) + kept_sum + out_bias
    pull_back = jax.vjp(layer_norm, residual, norm_gain, norm_shift)[1]
    grad_resid, grad_gain, grad_shift = pull_back(grad_out)
    grad_bias = jnp.sum(grad_resid, axis=(0, 1))
    branch_low = lax.all_gather(grad_resid.astype(jnp.bfloat16), "mp", axis=1, tiled=True)
    grad_part, grad_first, grad_down = branch_grad(
        branch_mode, whole_rows, segment, w_first, w_down, branch_low
    )
    grad_hidden = grad_resid + jax.tree.map(
        lambda part: part.astype(jnp.float32),
        lax.psum_scatter(as_sent(grad_part), "mp", scatter_dimension=1, tiled=True),
    )
    return (grad_hidden, (grad_first, grad_down, grad_bias, grad_gain, grad_shift))


def forward_pass(section_kind, chosen, encoders, hidden_in, segments, member_local, counts):
    section_index = lax.axis_index("section")
    section_count = lax.axis_size("section")
    row_count = hidden_in.shape[0] // MICRO
    local_shape = (row_count,) + hidden_in.shape[1:]
    arriving = jnp.zeros((len(chosen),) + local_shape, jnp.bfloat16)
    kept_inputs = jnp.zeros((MICRO,) + local_shape, jnp.bfloat16)
    kept_sums = jnp.zeros((MICRO,) + local_shape, jnp.float32)
    pooled = jnp.zeros(
        (len(chosen), MICRO, row_count, counts.shape[1], hidden_in.shape[2]), jnp.float32
    )
    for moment in range(MICRO + section_count - 1):
        micro_index = moment - section_index
        is_valid = (micro_index >= 0) & (micro_index < MICRO)
        slot_index = jnp.clip(micro_index, 0, MICRO - 1)
        branch_mode = jnp.where(is_valid, section_kind + 1, 0)
        segment = lax.dynamic_slice_in_dim(segments, slot_index * row_count, row_count, 0)
        member = lax.dynamic_slice_in_dim(member_local, slot_index * row_count, row_count, 0)
        crop_counts = lax.dynamic_slice_in_dim(counts, slot_index * row_count, row_count, 0)
        if moment < MICRO:
            fresh_rows = hidden_in[moment * row_count : (moment + 1) * row_count]
        else:
            fresh_rows = jnp.zeros(local_shape, jnp.bfloat16)
        at_last = is_valid & (section_index == section_count - 1)
        outgoing = []
        for position, encoder_id in enumerate(chosen):
            current = jnp.where(section_index == 0, fresh_rows, arriving[position])
            produced, combined = section_forward(
                branch_mode, current, segment, encoders[encoder_id]
            )
            if encoder_id == 0:
                kept_inputs = jnp.where(
                    is_valid,
                    lax.dynamic_update_index_in_dim(kept_inputs, current, slot_index, 0),
                    kept_inputs,
                )
                kept_sums = jnp.where(
                    is_valid,
                    lax.dynamic_update_index_in_dim(kept_sums, combined, slot_index, 0),
                    kept_sums,
                )
            crop_share = (
                jnp.einsum("rsc,rsd->rcd", member, produced, precision=lax.Precision.HIGHEST)
                / crop_counts[:, :, None]
            )
            pooled = pooled.at[position].set(
                jnp.where(
                    at_last,
                    lax.dynamic_update_index_in_dim(pooled[position], crop_share, slot_index, 0),
                    pooled[position],
                )
            )
            outgoing.append(produced.astype(jnp.bfloat16))
        arriving = shifted(jnp.stack(outgoing), "section", 1)
    return (kept_inputs, kept_sums, pooled)


def backward_pass(section_kind, weights, kept_inputs, kept_sums, segments, top_grads):
    section_index = lax.axis_index("section")
    section_count = lax.axis_size("section")
    row_count = kept_inputs.shape[1]
    arriving = jnp.zeros(kept_inputs.shape[1:], jnp.bfloat16)
    grad_inputs = jnp.zeros(kept_inputs.shape, jnp.float32)
    totals = tuple((jnp.zeros(piece.shape, jnp.float32) for piece in weights))
    for moment in range(MICRO + section_count - 1):
        micro_index = moment - (section_count - 1 - section_index)
        is_valid = (micro_index >= 0) & (micro_index < MICRO)
        slot_index = jnp.clip(micro_index, 0, MICRO - 1)
        branch_mode = jnp.where(is_valid, section_kind + 1, 0)
        segment = lax.dynamic_slice_in_dim(segments, slot_index * row_count, row_count, 0)
        current = lax.dynamic_index_in_dim(kept_inputs, slot_index, 0, keepdims=False)
        from_head = lax.dynamic_index_in_dim(top_grads, slot_index, 0, keepdims=False)
        kept_sum = lax.dynamic_index_in_dim(kept_sums, slot_index, 0, keepdims=False)
        grad_out = jnp.where(
            section_index == section_count - 1, from_head, arriving.astype(jnp.float32)
        )
        grad_hidden, increments = section_backward(
            branch_mode, current, segment, weights, grad_out, kept_sum
        )
        totals = jax.tree.map(
            lambda running, addend: running + jnp.where(is_valid, addend, 0.0), totals, increments
        )
        at_first = is_valid & (section_index == 0)
        grad_inputs = jnp.where(
            at_first,
            lax.dynamic_update_index_in_dim(grad_inputs, grad_hidden, slot_index, 0),
            grad_inputs,
        )
        arriving = shifted(grad_hidden.astype(jnp.bfloat16), "section", -1)
    return (grad_inputs, totals)


def crop_head(pooled_query, pooled_key, partners, queue):
    section_count = lax.axis_size("section")
    data_count = lax.axis_size("dp")
    core_count = lax.axis_size("mp")
    seg_count = partners.shape[1]
    model_width = pooled_query.shape[-1]
    query_share = pooled_query.reshape(-1, seg_count, model_width)
    key_share = pooled_key.reshape(-1, seg_count, model_width)
    pick_table = (
        partners[:, :, None] == jnp.arange(seg_count, dtype=jnp.int32)[None, None, :]
    ).astype(jnp.float32)
    partner_share = jnp.einsum(
        "rcp,rpd->rcd", pick_table, key_share, precision=lax.Precision.HIGHEST
    )
    own_count = query_share.shape[0] * seg_count
    sent_pair = jnp.stack(
        [query_share.reshape(own_count, model_width), partner_share.reshape(own_count, model_width)]
    )
    sent_pair = spread_2(sent_pair.astype(jnp.bfloat16), "section", section_count - 1).astype(
        sent_pair.dtype
    )
    every_pair = lax.all_gather(
        sent_pair.astype(jnp.bfloat16), ("dp", "mp"), axis=1, tiled=True
    ).astype(sent_pair.dtype)
    summed_pair = jnp.sum(
        every_pair.reshape(2, data_count, core_count, own_count, model_width), axis=2
    )
    query_full = summed_pair[0].reshape(-1, model_width)
    partner_full = summed_pair[1].reshape(-1, model_width)
    query_low = unit_rows(query_full).astype(jnp.bfloat16)
    partner_low = unit_rows(partner_full).astype(jnp.bfloat16)
    pos_logit = (
        jnp.sum(query_low.astype(jnp.float32) * partner_low.astype(jnp.float32), axis=-1) * inv_tau
    )
    queue_low = unit_rows(queue.astype(jnp.float32)).astype(jnp.bfloat16)
    neg_logit = (
        jnp.einsum("cd,jd->cj", query_low, queue_low, preferred_element_type=jnp.float32) * inv_tau
    )
    neg_weight = jnp.exp(neg_logit - inv_tau)
    partial_total = jnp.sum(neg_weight, axis=-1)
    partial_pull = jnp.dot(
        neg_weight, queue_low.astype(jnp.float32), precision=lax.Precision.HIGHEST
    )
    queue_total, queue_pull = lax.psum((partial_total, partial_pull), ("section", "dp", "mp"))
    denominator = jnp.exp(pos_logit - inv_tau) + queue_total
    log_total = inv_tau + jnp.log(denominator)
    loss_value = jnp.mean(log_total - pos_logit)
    start_row = lax.axis_index("dp") * own_count
    own_denominator = take_own(denominator, start_row, own_count)
    pos_weight = take_own(jnp.exp(pos_logit - inv_tau), start_row, own_count) / own_denominator
    own_partner = take_own(partner_low, start_row, own_count).astype(jnp.float32)
    own_pull = take_own(queue_pull, start_row, own_count)
    grad_query = (
        own_pull / own_denominator[:, None] + (pos_weight - 1.0)[:, None] * own_partner
    ) * (inv_tau / query_full.shape[0])
    pull_back = jax.vjp(unit_rows, take_own(query_full, start_row, own_count))[1]
    grad_pooled = pull_back(grad_query)[0]
    return (loss_value, grad_pooled.reshape(query_share.shape))


def local(
    hidden_in, segments, partners, queue, first_weight, second_weight, out_bias, ln_gain, ln_bias
):
    section_kind = lax.axis_index("section") % 2
    neighbour = shifted(second_weight, "section", 1)
    down_full = jnp.concatenate([neighbour[:, 0], second_weight[:, 0]], axis=1)
    encoders = [
        (
            first_weight[encoder_id, 0],
            down_full[encoder_id],
            out_bias[encoder_id, 0],
            ln_gain[encoder_id, 0],
            ln_bias[encoder_id, 0],
        )
        for encoder_id in range(2)
    ]
    local_len = hidden_in.shape[1]
    local_segments = lax.dynamic_slice_in_dim(
        segments, lax.axis_index("mp") * local_len, local_len, 1
    )
    crop_ids = jnp.arange(partners.shape[1], dtype=jnp.int32)
    member_local = (local_segments[:, :, None] == crop_ids).astype(jnp.float32)
    counts = jnp.sum((segments[:, :, None] == crop_ids).astype(jnp.float32), axis=1)
    kept_inputs, kept_sums, pooled = forward_pass(
        section_kind, (0,), encoders, hidden_in, segments, member_local, counts
    )
    pooled_query = pooled[0]
    pooled_key = forward_pass(
        section_kind, (1,), encoders, hidden_in, segments, member_local, counts
    )[2][0]
    loss_value, grad_pooled = crop_head(pooled_query, pooled_key, partners, queue)
    grad_tokens = jnp.einsum(
        "rsc,rcd->rsd",
        member_local,
        grad_pooled / counts[:, :, None],
        precision=lax.Precision.HIGHEST,
    )
    top_grads = grad_tokens.reshape(kept_inputs.shape)
    grad_inputs, totals = backward_pass(
        section_kind, encoders[0], kept_inputs, kept_sums, segments, top_grads
    )
    grad_first, grad_down, grad_bias, grad_gain, grad_shift = totals
    returned = shifted(as_sent(grad_down[:2]), "section", -1)
    grad_second = jnp.where(section_kind == 0, returned, grad_down[2:])
    grad_first, grad_second = (
        lax.psum(grad_first.astype(jnp.bfloat16), "dp").astype(jnp.float32),
        lax.psum(grad_second.astype(jnp.bfloat16), "dp").astype(jnp.float32),
    )
    grad_bias, grad_gain, grad_shift = lax.psum((grad_bias, grad_gain, grad_shift), ("dp", "mp"))
    grad_input = lax.psum_scatter(
        grad_inputs.reshape(hidden_in.shape).astype(jnp.bfloat16),
        "section",
        scatter_dimension=2,
        tiled=True,
    )
    return (
        loss_value,
        grad_input,
        grad_first[None],
        grad_second[None],
        grad_bias[None],
        grad_gain[None],
        grad_shift[None],
    )


def solution(mesh):
    in_specs = (
        P("dp", "mp", None),
        P("dp", None),
        P("dp", None),
        P(("section", "dp", "mp"), None),
        P(None, "section", None, None, "mp"),
        P(None, "section", None, "mp", None),
        P(None, "section", None),
        P(None, "section", None),
        P(None, "section", None),
    )
    out_specs = (
        P(),
        P("dp", "mp", "section"),
        P("section", None, None, "mp"),
        P("section", None, "mp", None),
        P("section", None),
        P("section", None),
        P("section", None),
    )
    return jax.shard_map(local, mesh=mesh, in_specs=in_specs, out_specs=out_specs, check_vma=False)
```

profile of v0, /device:TPU:2, one launch (start us, length us, event | category | flops | bytes accessed | tf_op | source)
XLA Modules:
  0.0 1743.0 jit_solution(6890099807725266362)
XLA Ops:
  21.9 40.5 %collective-permute-done = bf16[2,1,2,384,768]{4,3,2,0,1:T(8,128)(2,1)} collective-permute-done((bf16[2,1,2,384,768]{4,3,2,0,1:T(8,128)(2,1)}, bf16[2,1,2,384,768]{4,3,2,0,1:T(8,128)(2,1)}, u32[]{:S(2)}, u32[]{:S(2)}) %collective-permute-start) | collective-permute-done | bytes 2359328 | tf_op jit(solution)/shard_map/ppermute | solution.py:27
  78.6 38.0 %reduce-scatter.26.cloned.1.call-done = bf16[1,256,768]{2,1,0:T(8,128)(2,1)} async-done(((bf16[1,512,768]{2,1,0:T(8,128)(2,1)}), bf16[1,256,768]{2,1,0:T(8,128)(2,1)}) %reduce-scatter.26.cloned.1.call-update) | async-done | bytes 393232 | tf_op jit(solution)/shard_map/reduce_scatter | solution.py:214
  116.6 44.6 %reduce-scatter.16.cloned.1.call-done = bf16[1,256,768]{2,1,0:T(8,128)(2,1)} async-done(((bf16[1,512,768]{2,1,0:T(8,128)(2,1)}), bf16[1,256,768]{2,1,0:T(8,128)(2,1)}) %reduce-scatter.16.cloned.1.call-update) | async-done | bytes 393232 | tf_op jit(solution)/shard_map/reduce_scatter | solution.py:214
  184.2 13.4 conditional.21
  202.3 42.2 %collective-permute-done.1 = bf16[1,1,256,768]{3,2,1,0:T(8,128)(2,1)S(1)} collective-permute-done((bf16[1,1,256,768]{3,2,1,0:T(8,128)(2,1)}, bf16[1,1,256,768]{3,2,1,0:T(8,128)(2,1)S(1)}, u32[]{:S(2)}, u32[]{:S(2)}) %collective-permute-start.1) | collective-permute-done | bytes 393248 | tf_op jit(solution)/shard_map/ppermute | solution.py:27
  248.9 13.1 conditional.16
  276.8 36.0 %reduce-scatter.18.cloned.1.call-done = bf16[1,256,768]{2,1,0:T(8,128)(2,1)} async-done(((bf16[1,512,768]{2,1,0:T(8,128)(2,1)}), bf16[1,256,768]{2,1,0:T(8,128)(2,1)}) %reduce-scatter.18.cloned.1.call-update) | async-done | bytes 393232 | tf_op jit(solution)/shard_map/reduce_scatter | solution.py:214
  314.7 11.8 collective-permute-done.6
  330.7 13.4 conditional.22
  347.5 26.5 %collective-permute-start.2 = (bf16[1,1,256,768]{3,2,1,0:T(8,128)(2,1)S(1)}, bf16[1,1,256,768]{3,2,1,0:T(8,128)(2,1)S(1)}, u32[]{:S(2)}, u32[]{:S(2)}) collective-permute-start(bf16[1,1,256,768]{3,2,1,0:T(8,128)(2,1)S(1)} %fusion.983), channel_id=1, source_target_pairs={{0,8},{8,16},{16,24},{1,9},{9,17},{17,25},{2,10},{10,18},{18,26},{... | collective-permute-start | bytes 1179656 | tf_op jit(solution)/shard_map/ppermute | solution.py:27
  386.4 13.3 conditional.17
  409.2 41.0 %collective-permute-start.7 = (bf16[1,1,256,768]{3,2,1,0:T(8,128)(2,1)}, bf16[1,1,256,768]{3,2,1,0:T(8,128)(2,1)}, u32[]{:S(2)}, u32[]{:S(2)}) collective-permute-start(bf16[1,1,256,768]{3,2,1,0:T(8,128)(2,1)} %fusion.979), channel_id=1, source_target_pairs={{0,8},{8,16},{16,24},{1,9},{9,17},{17,25},{2,10},{10,18},{18,26},{... | collective-permute-start | bytes 1179656 | tf_op jit(solution)/shard_map/ppermute | solution.py:27
  467.5 52.7 %collective-permute-start.3 = (bf16[1,1,256,768]{3,2,1,0:T(8,128)(2,1)S(1)}, bf16[1,1,256,768]{3,2,1,0:T(8,128)(2,1)S(1)}, u32[]{:S(2)}, u32[]{:S(2)}) collective-permute-start(bf16[1,1,256,768]{3,2,1,0:T(8,128)(2,1)S(1)} %fusion.982), channel_id=1, source_target_pairs={{0,8},{8,16},{16,24},{1,9},{9,17},{17,25},{2,10},{10,18},{18,26},{... | collective-permute-start | bytes 1179656 | tf_op jit(solution)/shard_map/ppermute | solution.py:27
  552.3 45.1 %collective-permute-start.8 = (bf16[1,1,256,768]{3,2,1,0:T(8,128)(2,1)}, bf16[1,1,256,768]{3,2,1,0:T(8,128)(2,1)}, u32[]{:S(2)}, u32[]{:S(2)}) collective-permute-start(bf16[1,1,256,768]{3,2,1,0:T(8,128)(2,1)} %fusion.978), channel_id=1, source_target_pairs={{0,8},{8,16},{16,24},{1,9},{9,17},{17,25},{2,10},{10,18},{18,26},{... | collective-permute-start | bytes 1179656 | tf_op jit(solution)/shard_map/ppermute | solution.py:27
  651.9 12.5 reduce-scatter.24.cloned.1.call-done
  675.1 16.7 psum.56
  691.8 14.3 all_gather.70
  716.2 42.7 %psum.57 = f32[48]{0:T(128)} all-reduce(f32[48]{0:T(128)} %get-tuple-element.2582), channel_id=1, replica_groups=mesh['section'=4,'dp'=4,'mp'=2] {'section','dp','mp'}, use_global_device_ids=true, to_apply=%region_108.109 | all-reduce | flops 48 | bytes 384 | tf_op jit(solution)/shard_map/psum | solution.py:380
  763.7 117.9 %all-reduce.7.cloned.1.call-done = f32[48,768]{1,0:T(8,128)} async-done(((f32[48,768]{1,0:T(8,128)}), f32[48,768]{1,0:T(8,128)}) %all-reduce.7.cloned.1.call-update) | async-done | bytes 147472 | tf_op jit(solution)/shard_map/psum | solution.py:380
  891.2 13.0 conditional.25
  908.8 30.1 %reduce-scatter.36.cloned.1.call-done = bf16[1,256,768]{2,1,0:T(8,128)(2,1)} async-done(((bf16[1,512,768]{2,1,0:T(8,128)(2,1)}), bf16[1,256,768]{2,1,0:T(8,128)(2,1)}) %reduce-scatter.36.cloned.1.call-update) | async-done | bytes 393232 | tf_op jit(solution)/shard_map/reduce_scatter | solution.py:240
  943.0 11.6 collective-permute-done.9
  961.1 13.2 conditional.26
  978.6 112.8 %reduce-scatter.38.cloned.1.call-done = bf16[1,256,768]{2,1,0:T(8,128)(2,1)} async-done(((bf16[1,512,768]{2,1,0:T(8,128)(2,1)}), bf16[1,256,768]{2,1,0:T(8,128)(2,1)}) %reduce-scatter.38.cloned.1.call-update) | async-done | bytes 393232 | tf_op jit(solution)/shard_map/reduce_scatter | solution.py:240
  1113.6 31.4 %conditional.27 = (bf16[1,512,768]{2,1,0:T(8,128)(2,1)}, f32[4,384,768]{2,1,0:T(8,128)}, f32[768,4,384]{2,1,0:T(4,128)}) conditional(s32[]{:T(128)} %clamp.42, () %tuple.334, (bf16[768,4,384]{2,0,1:T(8,128)(2,1)S(1)}, bf16[1,512,768]{2,1,0:T(8,128)(2,1)}, s32[2,512]{1,0:T(2,128)S(1)}, s32[]{:T(128)}, ...), branch_computations={%region_143.144_spmd, %region_144.150_spmd, %region_150.151_spmd} | conditional | flops 6115688448 | bytes 88936488 | solution.py:200
  1149.3 95.3 %reduce-scatter.40.cloned.1.call-done = bf16[1,256,768]{2,1,0:T(8,128)(2,1)} async-done(((bf16[1,512,768]{2,1,0:T(8,128)(2,1)}), bf16[1,256,768]{2,1,0:T(8,128)(2,1)}) %reduce-scatter.40.cloned.1.call-update) | async-done | bytes 393232 | tf_op jit(solution)/shard_map/reduce_scatter | solution.py:240
  1266.8 31.0 %conditional.28 = (bf16[1,512,768]{2,1,0:T(8,128)(2,1)}, f32[4,384,768]{2,1,0:T(8,128)}, f32[768,4,384]{2,1,0:T(4,128)}) conditional(s32[]{:T(128)} %clamp.43, () %tuple.337, (bf16[768,4,384]{2,0,1:T(8,128)(2,1)S(1)}, bf16[1,512,768]{2,1,0:T(8,128)(2,1)}, s32[2,512]{1,0:T(2,128)S(1)}, s32[]{:T(128)}, ...), branch_computations={%region_156.157_spmd, %region_157.163_spmd, %region_163.164_spmd} | conditional | flops 6115688448 | bytes 88936488 | solution.py:200
  1305.4 91.1 %reduce-scatter.42.cloned.1.call-done = bf16[1,256,768]{2,1,0:T(8,128)(2,1)} async-done(((bf16[1,512,768]{2,1,0:T(8,128)(2,1)}), bf16[1,256,768]{2,1,0:T(8,128)(2,1)}) %reduce-scatter.42.cloned.1.call-update) | async-done | bytes 393232 | tf_op jit(solution)/shard_map/reduce_scatter | solution.py:240
  1440.8 91.1 %collective-permute-start.13 = (bf16[2,384,768]{2,1,0:T(8,128)(2,1)}, bf16[2,384,768]{2,1,0:T(8,128)(2,1)}, u32[]{:S(2)}, u32[]{:S(2)}) collective-permute-start(bf16[2,384,768]{2,1,0:T(8,128)(2,1)} %slice.777), channel_id=1, source_target_pairs={{8,0},{16,8},{24,16},{9,1},{17,9},{25,17},{10,2},{18,10},{26,18},{... | collective-permute-start | bytes 3538952 | tf_op jit(solution)/shard_map/ppermute | solution.py:27
  1545.2 19.0 %collective-permute-done.13 = bf16[2,384,768]{2,1,0:T(8,128)(2,1)} collective-permute-done((bf16[2,384,768]{2,1,0:T(8,128)(2,1)}, bf16[2,384,768]{2,1,0:T(8,128)(2,1)}, u32[]{:S(2)}, u32[]{:S(2)}) %collective-permute-start.13) | collective-permute-done | bytes 1179680 | tf_op jit(solution)/shard_map/ppermute | solution.py:27
  1568.9 16.9 all-reduce.1
  1593.0 135.3 %all-reduce.11.cloned.1.call-done = (bf16[1,768,4,384]{3,2,1,0:T(4,128)(2,1)}, bf16[1,2,384,768]{3,2,1,0:T(8,128)(2,1)}) async-done(((bf16[1,768,4,384]{3,2,1,0:T(4,128)(2,1)}, bf16[1,2,384,768]{3,2,1,0:T(8,128)(2,1)}), (bf16[1,768,4,384]{3,2,1,0:T(4,128)(2,1)}, bf16[1,2,384,768]{3,2,1,0:T(8,128)(2,1)})) %all-reduce.11.cloned.1.call-update) | async-done | bytes 3538960 | tf_op jit(solution)/shard_map/psum | solution.py:442
  (515 shorter events, 534.3 us)
Async XLA Ops:
  7.2 109.5 %reduce-scatter.26.cloned.1.call-start = ((), (), s32[]{:S(2)}) async-start(), calls=%async_computation.20 | async-start | bytes 1179648 | tf_op jit(solution)/shard_map/reduce_scatter | solution.py:214
  7.2 55.2 %collective-permute-start = (bf16[2,1,2,384,768]{4,3,2,0,1:T(8,128)(2,1)}, bf16[2,1,2,384,768]{4,3,2,0,1:T(8,128)(2,1)}, u32[]{:S(2)}, u32[]{:S(2)}) collective-permute-start(bf16[2,1,2,384,768]{4,3,2,0,1:T(8,128)(2,1)} %bitcast.1613), channel_id=1, source_target_pairs={{0,8},{8,16},{16,24},{1,9},{9,17},{17,25},{2,10},{10,18},{18,26},{... | collective-permute-start | bytes 7077896 | tf_op jit(solution)/shard_map/ppermute | solution.py:27
  67.0 94.2 %reduce-scatter.16.cloned.1.call-start = ((), (), s32[]{:S(2)}) async-start(), calls=%async_computation.15 | async-start | bytes 1179648 | tf_op jit(solution)/shard_map/reduce_scatter | solution.py:214
  76.5 190.8 %reduce-scatter.28.cloned.1.call-start = ((), (), s32[]{:S(2)}) async-start(), calls=%async_computation.21 | async-start | bytes 1179648 | tf_op jit(solution)/shard_map/reduce_scatter | solution.py:214
  167.0 13.5 collective-permute-start.5
  197.6 115.1 %reduce-scatter.18.cloned.1.call-start = ((), (), s32[]{:S(2)}) async-start(), calls=%async_computation.16 | async-start | bytes 1179648 | tf_op jit(solution)/shard_map/reduce_scatter | solution.py:214
  199.2 45.3 %collective-permute-start.1 = (bf16[1,1,256,768]{3,2,1,0:T(8,128)(2,1)}, bf16[1,1,256,768]{3,2,1,0:T(8,128)(2,1)S(1)}, u32[]{:S(2)}, u32[]{:S(2)}) collective-permute-start(bf16[1,1,256,768]{3,2,1,0:T(8,128)(2,1)} %get-tuple-element.2569), channel_id=1, source_target_pairs={{0,8},{8,16},{16,24},{1,9},{9,17},{17,25},{2,10},{10,18},{18,26},{... | collective-permute-start | bytes 1179656 | tf_op jit(solution)/shard_map/ppermute | solution.py:27
  262.1 142.2 %reduce-scatter.30.cloned.1.call-start = ((), (), s32[]{:S(2)}) async-start(), calls=%async_computation.22 | async-start | bytes 1179648 | tf_op jit(solution)/shard_map/reduce_scatter | solution.py:214
  271.9 54.5 %collective-permute-start.6 = (bf16[1,1,256,768]{3,2,1,0:T(8,128)(2,1)}, bf16[1,1,256,768]{3,2,1,0:T(8,128)(2,1)}, u32[]{:S(2)}, u32[]{:S(2)}) collective-permute-start(bf16[1,1,256,768]{3,2,1,0:T(8,128)(2,1)} %fusion.977), channel_id=1, source_target_pairs={{0,8},{8,16},{16,24},{1,9},{9,17},{17,25},{2,10},{10,18},{18,26},{... | collective-permute-start | bytes 1179656 | tf_op jit(solution)/shard_map/ppermute | solution.py:27
  344.1 108.4 %reduce-scatter.20.cloned.1.call-start = ((), (), s32[]{:S(2)}) async-start(), calls=%async_computation.17 | async-start | bytes 1179648 | tf_op jit(solution)/shard_map/reduce_scatter | solution.py:214
  347.5 35.4 %collective-permute-start.2 = (bf16[1,1,256,768]{3,2,1,0:T(8,128)(2,1)S(1)}, bf16[1,1,256,768]{3,2,1,0:T(8,128)(2,1)S(1)}, u32[]{:S(2)}, u32[]{:S(2)}) collective-permute-start(bf16[1,1,256,768]{3,2,1,0:T(8,128)(2,1)S(1)} %fusion.983), channel_id=1, source_target_pairs={{0,8},{8,16},{16,24},{1,9},{9,17},{17,25},{2,10},{10,18},{18,26},{... | collective-permute-start | bytes 1179656 | tf_op jit(solution)/shard_map/ppermute | solution.py:27
  399.7 147.7 %reduce-scatter.32.cloned.1.call-start = ((), (), s32[]{:S(2)}) async-start(), calls=%async_computation.23 | async-start | bytes 1179648 | tf_op jit(solution)/shard_map/reduce_scatter | solution.py:214
  409.2 50.0 %collective-permute-start.7 = (bf16[1,1,256,768]{3,2,1,0:T(8,128)(2,1)}, bf16[1,1,256,768]{3,2,1,0:T(8,128)(2,1)}, u32[]{:S(2)}, u32[]{:S(2)}) collective-permute-start(bf16[1,1,256,768]{3,2,1,0:T(8,128)(2,1)} %fusion.979), channel_id=1, source_target_pairs={{0,8},{8,16},{16,24},{1,9},{9,17},{17,25},{2,10},{10,18},{18,26},{... | collective-permute-start | bytes 1179656 | tf_op jit(solution)/shard_map/ppermute | solution.py:27
  464.4 133.1 %reduce-scatter.22.cloned.1.call-start = ((), (), s32[]{:S(2)}) async-start(), calls=%async_computation.18 | async-start | bytes 1179648 | tf_op jit(solution)/shard_map/reduce_scatter | solution.py:214
  467.5 61.4 %collective-permute-start.3 = (bf16[1,1,256,768]{3,2,1,0:T(8,128)(2,1)S(1)}, bf16[1,1,256,768]{3,2,1,0:T(8,128)(2,1)S(1)}, u32[]{:S(2)}, u32[]{:S(2)}) collective-permute-start(bf16[1,1,256,768]{3,2,1,0:T(8,128)(2,1)S(1)} %fusion.982), channel_id=1, source_target_pairs={{0,8},{8,16},{16,24},{1,9},{9,17},{17,25},{2,10},{10,18},{18,26},{... | collective-permute-start | bytes 1179656 | tf_op jit(solution)/shard_map/ppermute | solution.py:27
  540.1 103.7 %reduce-scatter.34.cloned.1.call-start = ((), (), s32[]{:S(2)}) async-start(), calls=%async_computation.24 | async-start | bytes 1179648 | tf_op jit(solution)/shard_map/reduce_scatter | solution.py:214
  552.3 54.1 %collective-permute-start.8 = (bf16[1,1,256,768]{3,2,1,0:T(8,128)(2,1)}, bf16[1,1,256,768]{3,2,1,0:T(8,128)(2,1)}, u32[]{:S(2)}, u32[]{:S(2)}) collective-permute-start(bf16[1,1,256,768]{3,2,1,0:T(8,128)(2,1)} %fusion.978), channel_id=1, source_target_pairs={{0,8},{8,16},{16,24},{1,9},{9,17},{17,25},{2,10},{10,18},{18,26},{... | collective-permute-start | bytes 1179656 | tf_op jit(solution)/shard_map/ppermute | solution.py:27
  611.7 52.8 %reduce-scatter.24.cloned.1.call-start = ((), (), s32[]{:S(2)}) async-start(), calls=%async_computation.19 | async-start | bytes 1179648 | tf_op jit(solution)/shard_map/reduce_scatter | solution.py:214
  613.7 14.7 collective-permute-start.4
  640.0 241.6 %all-reduce.7.cloned.1.call-start = ((), (), s32[]{:S(2)}) async-start(), calls=%async_computation.25 | async-start | bytes 294912 | tf_op jit(solution)/shard_map/psum | solution.py:380
  761.4 177.5 %reduce-scatter.36.cloned.1.call-start = ((), (), s32[]{:S(2)}) async-start(), calls=%async_computation.26 | async-start | bytes 1179648 | tf_op jit(solution)/shard_map/reduce_scatter | solution.py:240
  904.3 187.1 %reduce-scatter.38.cloned.1.call-start = ((), (), s32[]{:S(2)}) async-start(), calls=%async_computation.27 | async-start | bytes 1179648 | tf_op jit(solution)/shard_map/reduce_scatter | solution.py:240
  940.5 14.1 collective-permute-start.9
  974.4 270.3 %reduce-scatter.40.cloned.1.call-start = ((), (), s32[]{:S(2)}) async-start(), calls=%async_computation.28 | async-start | bytes 1179648 | tf_op jit(solution)/shard_map/reduce_scatter | solution.py:240
  1092.9 14.1 collective-permute-start.10
  1145.1 251.4 %reduce-scatter.42.cloned.1.call-start = ((), (), s32[]{:S(2)}) async-start(), calls=%async_computation.29 | async-start | bytes 1179648 | tf_op jit(solution)/shard_map/reduce_scatter | solution.py:240
  1246.1 14.1 collective-permute-start.11
  1297.9 234.0 %reduce-scatter.44.cloned.1.call-start = ((), (), s32[]{:S(2)}) async-start(), calls=%async_computation.30 | async-start | bytes 1179648 | tf_op jit(solution)/shard_map/reduce_scatter | solution.py:240
  1398.0 14.3 collective-permute-start.12
  1427.6 163.7 %all-reduce.9.cloned.1.call-start = ((), (), s32[]{:S(2)}) async-start(), calls=%async_computation.31 | async-start | bytes 1572864
  1440.8 123.4 %collective-permute-start.13 = (bf16[2,384,768]{2,1,0:T(8,128)(2,1)}, bf16[2,384,768]{2,1,0:T(8,128)(2,1)}, u32[]{:S(2)}, u32[]{:S(2)}) collective-permute-start(bf16[2,384,768]{2,1,0:T(8,128)(2,1)} %slice.777), channel_id=1, source_target_pairs={{8,0},{16,8},{24,16},{9,1},{17,9},{25,17},{10,2},{18,10},{26,18},{... | collective-permute-start | bytes 3538952 | tf_op jit(solution)/shard_map/ppermute | solution.py:27
  1537.6 190.8 %all-reduce.11.cloned.1.call-start = ((), (), s32[]{:S(2)}) async-start(), calls=%async_computation.32 | async-start | bytes 7077888 | tf_op jit(solution)/shard_map/psum | solution.py:442
  (100 other events, 2646.7 us)
Sparse Core Ops, SparseCore 0:
  67.1 49.4 reduce-scatter.25
  119.0 42.2 reduce-scatter.15
  197.8 41.4 reduce-scatter.27
  262.2 50.5 reduce-scatter.17
  344.3 31.6 reduce-scatter.29
  399.8 46.0 reduce-scatter.19
  464.5 57.8 reduce-scatter.31
  540.2 50.1 reduce-scatter.21
  611.8 21.6 reduce-scatter.33
  640.1 24.2 reduce-scatter.23
  761.5 120.0 all-reduce.6
  904.4 34.4 reduce-scatter.35
  974.5 116.8 reduce-scatter.37
  1145.2 99.3 reduce-scatter.39
  1298.0 98.4 reduce-scatter.41
  1427.7 96.3 reduce-scatter.43
  1537.7 53.5 all-reduce.8
  1594.1 134.1 all-reduce.10
where the time goes:
time: 1760 us; the launch traced here: 1740 us
  waiting for transfers between devices  904 us (51%)
  starting transfers between devices  282 us (16%)
  blocking collectives  146 us (8%)
  other arithmetic  145 us (8%)
  matrix products  116 us (7%)
  local copies, waits for them, and re-layouts  85.9 us (5%)
  loops' own time  44.1 us (3%)
  between operations  19 us (1%)
    reduce_scatter x5, waiting for transfers between devices, section_backward(): lax.psum_scatter(as_sent(grad_part), 'mp', scatter_dimension=1, tiled=True)  329 us
    ppermute x14, starting transfers between devices, shifted(): return lax.ppermute(shard, axis, pairs)  281 us
    ppermute x14, waiting for transfers between devices, shifted(): return lax.ppermute(shard, axis, pairs)  185 us
    psum x1, waiting for transfers between devices, local(): lax.psum(grad_first.astype(jnp.bfloat16), 'dp').astype(jnp.float32)  135 us
    reduce_scatter x10, waiting for transfers between devices, narrow(): lax.psum_scatter(as_sent(partial_value), 'mp', scatter_dimension=1, tiled...  131 us
    psum x1, waiting for transfers between devices, crop_head(): lax.psum((partial_total, partial_pull), ('section', 'dp', 'mp'))  118 us
    psum x1, blocking collectives, crop_head(): lax.psum((partial_total, partial_pull), ('section', 'dp', 'mp'))  42.7 us
    all_gather x14, blocking collectives, widen_rows(): return lax.all_gather(local_rows, 'mp', axis=1, tiled=True)  41.9 us
  transfers between devices with their start and end apart: 32, of which 24 were waited for; matrix products, arithmetic and copies ran while one was open for 9% of the time, Pallas kernels for 0%

commit v1 on v0

v1 whole, which is shorter than its diff:
```python
import functools
import jax
import jax.numpy as jnp
from jax import lax
from jax.experimental import pallas as pl
from jax.experimental.pallas import tpu as pltpu

F32 = jnp.float32
BF = jnp.bfloat16
HD = 64
NEG = -1e30
LN_EPS = 1e-12


def mm(a, b, ca=1, cb=0):
    return lax.dot_general(a, b, (((ca,), (cb,)), ((), ())), preferred_element_type=F32)


def norm_rows(resid, gain, shift):
    centre = resid - jnp.mean(resid, axis=-1, keepdims=True)
    spread = jnp.mean(centre * centre, axis=-1, keepdims=True)
    rstd = lax.rsqrt(spread + LN_EPS)
    xhat = centre * rstd
    return xhat * gain + shift, xhat, rstd


def norm_back(g, xhat, rstd, gain):
    gg = g * gain
    m1 = jnp.mean(gg, axis=-1, keepdims=True)
    m2 = jnp.mean(gg * xhat, axis=-1, keepdims=True)
    return rstd * (gg - m1 - xhat * m2)


def lane_low(shape):
    return lax.broadcasted_iota(jnp.int32, shape, len(shape) - 1) < HD


def qkv_rows(x, w_ref, qkv_ref, row0, rows):
    for h in range(2):
        n = qkv_ref.shape[2]
        qkv_ref[h, pl.ds(row0, rows), :] = mm(x, w_ref[h, :, :n]).astype(BF)


def attend_rows(qkv_ref, seg_col, seg_row, p_ref, mixed_ref, row0, rows):
    half = qkv_ref.shape[2] // 3
    pairs = half // 128
    same = seg_col == seg_row
    low = lane_low((rows, 128))
    for h in range(2):
        for pp in range(pairs):
            q = qkv_ref[h, pl.ds(row0, rows), pl.ds(pp * 128, 128)]
            k = qkv_ref[h, :, pl.ds(half + pp * 128, 128)]
            v = qkv_ref[h, :, pl.ds(2 * half + pp * 128, 128)]
            outs = []
            for a in range(2):
                qa = jnp.where(low if a == 0 else ~low, q, jnp.zeros_like(q))
                s = mm(qa, k, 1, 1) * (HD ** -0.5)
                s = jnp.where(same, s, NEG)
                mx = jnp.max(s, axis=-1, keepdims=True)
                e = jnp.exp(s - mx)
                p = (e * (1.0 / jnp.sum(e, axis=-1, keepdims=True))).astype(BF)
                if p_ref is not None:
                    p_ref[(h * pairs + pp) * 2 + a, pl.ds(row0, rows), :] = p
                outs.append(mm(p, v))
            mixed_ref[pl.ds(row0, rows), pl.ds(h * half + pp * 128, 128)] = jnp.where(
                low, outs[0], outs[1]
            ).astype(BF)


def attn_out(mixed, w_ref, n_qkv):
    half = mixed.shape[1] // 2
    return mm(mixed[:, :half], w_ref[0, :, n_qkv:], 1, 1) + mm(
        mixed[:, half:], w_ref[1, :, n_qkv:], 1, 1
    )


def gelu_parts(up, want_slope):
    cdf = 0.5 * (1.0 + lax.erf(up * (0.5 ** 0.5)))
    act = up * cdf
    if not want_slope:
        return act, None
    slope = cdf + up * (jnp.exp(-0.5 * up * up) * 0.3989422804014327)
    return act, slope


def ffn_rows(x, w_ref, v_ref, act_ref, slope_ref, row0, rows, tile=512):
    acc = None
    for h in range(2):
        n = w_ref.shape[2]
        for c in range(0, n, tile):
            up = mm(x, w_ref[h, :, c : c + tile])
            act, slope = gelu_parts(up, slope_ref is not None)
            act = act.astype(BF)
            if slope_ref is not None:
                act_ref[h, pl.ds(row0, rows), c : c + tile] = act
                slope_ref[h, pl.ds(row0, rows), c : c + tile] = slope.astype(BF)
            part = mm(act, v_ref[h, c : c + tile, :])
            acc = part if acc is None else acc + part
    return acc


def ffn_back_rows(low, w_ref, v_ref, slope_ref, gup_ref, row0, rows, tile=512):
    acc = None
    for h in range(2):
        n = w_ref.shape[2]
        for c in range(0, n, tile):
            dact = mm(low, v_ref[h, c : c + tile, :], 1, 1)
            gup = (dact * slope_ref[h, pl.ds(row0, rows), c : c + tile].astype(F32)).astype(BF)
            gup_ref[h, pl.ds(row0, rows), c : c + tile] = gup
            part = mm(gup, w_ref[h, :, c : c + tile], 1, 1)
            acc = part if acc is None else acc + part
    return acc


def attn_back_core(low_ref, w_ref, qkv_ref, p_ref, dqkv_ref, n_qkv):
    half = n_qkv // 3
    pairs = half // 128
    seq = low_ref.shape[0]
    low = lane_low((seq, 128))
    for h in range(2):
        for pp in range(pairs):
            gm = mm(low_ref[...], w_ref[h, :, n_qkv + pp * 128 : n_qkv + pp * 128 + 128]).astype(BF)
            q = qkv_ref[h, :, pl.ds(pp * 128, 128)]
            k = qkv_ref[h, :, pl.ds(half + pp * 128, 128)]
            v = qkv_ref[h, :, pl.ds(2 * half + pp * 128, 128)]
            dq, dk, dv = [], [], []
            for a in range(2):
                keep = low if a == 0 else ~low
                gma = jnp.where(keep, gm, jnp.zeros_like(gm))
                pb = p_ref[(h * pairs + pp) * 2 + a, :, :]
                g = mm(gma, v, 1, 1)
                pf = pb.astype(F32)
                rs = jnp.sum(pf * g, axis=-1, keepdims=True)
                ds = (pf * (g - rs)).astype(BF)
                dq.append(mm(ds, k))
                dk.append(mm(ds, q, 0, 0))
                dv.append(mm(pb, gm, 0, 0))
            sc = HD ** -0.5
            dqkv_ref[h, :, pl.ds(pp * 128, 128)] = (jnp.where(low, dq[0], dq[1]) * sc).astype(BF)
            dqkv_ref[h, :, pl.ds(half + pp * 128, 128)] = (jnp.where(low, dk[0], dk[1]) * sc).astype(BF)
            dqkv_ref[h, :, pl.ds(2 * half + pp * 128, 128)] = jnp.where(low, dv[0], dv[1]).astype(BF)


from jax.sharding import PartitionSpec as P

MESH = pl.DeviceIdType.MESH
inv_tau = 20.0
unit_eps = 1e-06
ROWS = 256
VMEM_BYTES = 62 * 2**20


def member_rows(seg_row, count):
    return (lax.broadcasted_iota(jnp.int32, (count, seg_row.shape[1]), 0) == seg_row).astype(F32)


def split_mm(member, value):
    high = value.astype(BF)
    rest = (value - high.astype(F32)).astype(BF)
    return mm(member, high) + mm(member, rest)


def forward_kernel(
    hid, w1, w2, segc, segr, small,
    o_qkv, o_p, o_mixed, o_act, o_slope, o_xhat, o_rstd, o_x, o_w, o_v, o_pool,
    W, V, X, Y, qkv, prob, mixed, act, slope, yf, xhat, rstd,
    l_sem, ws, wr, vbs, vbr, vas, var, vfs, vfr, hs, hr, acs, acr, o_sem,
):
    s, m = lax.axis_index("section"), lax.axis_index("mp")
    last = lax.axis_size("section") - 1
    other = 1 - m
    seq = X.shape[1]
    chunks = seq // ROWS
    n_qkv = qkv.shape[3]
    va_rows = w2.shape[1]
    even = lax.rem(s, 2) == 0
    odd = lax.rem(s, 2) == 1

    barrier = pltpu.get_barrier_semaphore()
    pl.semaphore_signal(barrier, inc=1, device_id={"mp": other}, device_id_type=MESH)

    @pl.when(s > 0)
    def _():
        pl.semaphore_signal(barrier, inc=1, device_id={"section": s - 1}, device_id_type=MESH)

    @pl.when(s < last)
    def _():
        pl.semaphore_signal(barrier, inc=1, device_id={"section": s + 1}, device_id_type=MESH)

    pl.semaphore_wait(barrier, 1 + jnp.where(s > 0, 1, 0) + jnp.where(s < last, 1, 0))

    def to_core(src, dst, ss, rs):
        return pltpu.make_async_remote_copy(
            src_ref=src, dst_ref=dst, send_sem=ss, recv_sem=rs,
            device_id={"mp": other}, device_id_type=MESH,
        )

    def to_next(src, dst, ss, rs):
        return pltpu.make_async_remote_copy(
            src_ref=src, dst_ref=dst, send_sem=ss, recv_sem=rs,
            device_id={"section": s + 1}, device_id_type=MESH,
        )

    def w_far(e):
        return to_core(w1.at[e], W.at[e, m], ws.at[e], wr.at[e])

    def w_near(e):
        return pltpu.make_async_copy(w1.at[e], W.at[e, m], l_sem.at[e])

    def vb_far(e):
        return to_core(w2.at[e], V.at[e, m, pl.ds(va_rows, va_rows)], vbs.at[e], vbr.at[e])

    def vb_near(e):
        return pltpu.make_async_copy(w2.at[e], V.at[e, m, pl.ds(va_rows, va_rows)], l_sem.at[2 + e])

    def va_next(e):
        return to_next(w2.at[e], V.at[e, m, pl.ds(0, va_rows)], vas.at[e], var.at[e])

    def va_core(e):
        part = V.at[e, m, pl.ds(0, va_rows)]
        return to_core(part, part, vfs.at[e], vfr.at[e])

    def hid_far(e):
        return to_core(hid.at[other], X.at[e, pl.ds(pl.multiple_of(m * ROWS, ROWS), ROWS)], hs.at[e], hr.at[e])

    def hid_near(e):
        return pltpu.make_async_copy(
            hid.at[m], X.at[e, pl.ds(pl.multiple_of(m * ROWS, ROWS), ROWS)], l_sem.at[4 + e]
        )

    def act_next(e, c):
        rows = pl.ds(pl.multiple_of(c * ROWS, ROWS), ROWS)
        return to_next(Y.at[e, rows], X.at[e, rows], acs.at[e, c], acr.at[e, c])

    @pl.when(s == 0)
    def _():
        for e in range(2):
            hid_far(e).start()
            hid_near(e).start()

    w_far(0).start()
    w_near(0).start()

    @pl.when(odd)
    def _():
        vb_far(0).start()
        vb_near(0).start()

    @pl.when(even)
    def _():
        va_next(0).start()

    w_far(1).start()
    w_near(1).start()

    @pl.when(odd)
    def _():
        vb_far(1).start()
        vb_near(1).start()

    @pl.when(s == 0)
    def _():
        for e in range(2):
            hid_far(e).wait_recv()
            hid_near(e).wait()

    def saves(e):
        pairs = [
            (qkv.at[0], o_qkv), (prob, o_p), (mixed.at[0], o_mixed), (act, o_act), (slope, o_slope),
            (xhat, o_xhat), (rstd, o_rstd), (X.at[0], o_x), (W.at[0], o_w), (V.at[0], o_v),
        ]
        return [pltpu.make_async_copy(a, b, o_sem.at[i]) for i, (a, b) in enumerate(pairs)]

    def finish(e, rows, resid):
        y, xh, rs = norm_rows(resid, small[e, 1:2, :], small[e, 2:3, :])
        if e == 0:
            xhat[rows, :] = xh
            rstd[rows, :] = jnp.broadcast_to(rs, (ROWS, 128))
        return y

    def wait_w(e):
        w_near(e).wait()
        w_far(e).wait_recv()

    def attention(e):
        wait_w(e)

        def project(c, carry):
            @pl.when(s > 0)
            def _():
                act_next(e, c).wait_recv()

            r = pl.multiple_of(c * ROWS, ROWS)
            qkv_rows(X[e, pl.ds(r, ROWS), :], W.at[e], qkv.at[e], r, ROWS)
            return carry

        lax.fori_loop(0, chunks, project, 0)

        def attend(c, carry):
            r = pl.multiple_of(c * ROWS, ROWS)
            rows = pl.ds(r, ROWS)
            attend_rows(qkv.at[e], segc[rows, :1], segr[:1, :], prob if e == 0 else None, mixed.at[e], r, ROWS)
            branch = attn_out(mixed[e, rows, :], W.at[e], n_qkv)
            y = finish(e, rows, X[e, rows, :].astype(F32) + branch + small[e, 0:1, :])
            Y[e, rows, :] = y.astype(BF)
            act_next(e, c).start()
            return carry

        lax.fori_loop(0, chunks, attend, 0)

    def feed(e):
        wait_w(e)
        va_next(e).wait_recv()
        va_core(e).start()
        vb_near(e).wait()
        vb_far(e).wait_recv()
        va_core(e).wait_recv()

        def one(c, carry):
            act_next(e, c).wait_recv()
            r = pl.multiple_of(c * ROWS, ROWS)
            rows = pl.ds(r, ROWS)
            x = X[e, rows, :]
            if e == 0:
                branch = ffn_rows(x, W.at[e], V.at[e], act, slope, r, ROWS)
            else:
                branch = ffn_rows(x, W.at[e], V.at[e], None, None, r, ROWS)
            y = finish(e, rows, x.astype(F32) + branch + small[e, 0:1, :])

            @pl.when(s < last)
            def _():
                Y[e, rows, :] = y.astype(BF)
                act_next(e, c).start()

            @pl.when(s == last)
            def _():
                yf[rows, :] = y

            return carry

        lax.fori_loop(0, chunks, one, 0)

        @pl.when(s == last)
        def _():
            member = member_rows(segr[:1, :], 8)
            counts = jnp.sum(member, axis=-1, keepdims=True)
            o_pool[e] = split_mm(member.astype(BF), yf[...]) / jnp.maximum(counts, 1.0)

    for e in range(2):
        @pl.when(even)
        def _():
            attention(e)
            if e == 0:
                va_next(1).start()

        @pl.when(odd)
        def _():
            feed(e)

        if e == 0:
            for copy in saves(0):
                copy.start()

    for copy in saves(0):
        copy.wait()
    for e in range(2):
        w_far(e).wait_send()

        @pl.when(odd)
        def _():
            vb_far(e).wait_send()
            va_core(e).wait_send()

        @pl.when(even)
        def _():
            va_next(e).wait_send()

        @pl.when(s == 0)
        def _():
            hid_far(e).wait_send()

        @pl.when(s < last)
        def _():
            for c in range(chunks):
                act_next(e, c).wait_send()


def backward_kernel(
    i_qkv, i_p, i_mixed, i_act, i_slope, i_xhat, i_rstd, i_x, i_w, i_v, gpool, segc, small,
    o_gin, o_dw, o_dv, o_sum,
    qkv, prob, mixed, act, slope, xhat, rstd, X, W, V, G, gout, low, resid, gup, dqkv, gsplit,
    i_sem, gs, gr, is_, ir,
):
    s, m = lax.axis_index("section"), lax.axis_index("mp")
    sections = lax.axis_size("section")
    last = sections - 1
    seq = X.shape[0]
    chunks = seq // ROWS
    n_qkv = qkv.shape[2]
    even = lax.rem(s, 2) == 0
    odd = lax.rem(s, 2) == 1
    loads = [
        pltpu.make_async_copy(a, b, i_sem.at[i])
        for i, (a, b) in enumerate(
            [(i_qkv, qkv), (i_p, prob), (i_mixed, mixed), (i_act, act), (i_slope, slope),
             (i_xhat, xhat), (i_rstd, rstd), (i_x, X), (i_w, W), (i_v, V)]
        )
    ]
    for copy in loads:
        copy.start()

    barrier = pltpu.get_barrier_semaphore()
    for t in range(sections):
        for c in range(2):
            @pl.when((s != t) | (m != c))
            def _():
                pl.semaphore_signal(barrier, inc=1, device_id={"section": t, "mp": c}, device_id_type=MESH)

    pl.semaphore_wait(barrier, 2 * sections - 1)

    def grad_prev(c):
        rows = pl.ds(pl.multiple_of(c * ROWS, ROWS), ROWS)
        return pltpu.make_async_remote_copy(
            src_ref=gout.at[rows], dst_ref=G.at[rows], send_sem=gs.at[c], recv_sem=gr.at[c],
            device_id={"section": s - 1}, device_id_type=MESH,
        )

    def spread(t, c):
        return pltpu.make_async_remote_copy(
            src_ref=gsplit.at[t, pl.ds(c * ROWS, ROWS)], dst_ref=o_gin.at[m],
            send_sem=is_.at[t * 2 + c], recv_sem=ir.at[m],
            device_id={"section": t, "mp": c}, device_id_type=MESH,
        )

    for copy in loads:
        copy.wait()

    o_sum[...] = jnp.zeros_like(o_sum)

    def through_norm(c, g):
        rows = pl.ds(pl.multiple_of(c * ROWS, ROWS), ROWS)
        xh = xhat[rows, :]
        grad = norm_back(g, xh, rstd[rows, :1], small[1:2, :])
        o_sum[0:1, :] += jnp.sum(grad, axis=0, keepdims=True)
        o_sum[1:2, :] += jnp.sum(g * xh, axis=0, keepdims=True)
        o_sum[2:3, :] += jnp.sum(g, axis=0, keepdims=True)
        resid[rows, :] = grad
        low[rows, :] = grad.astype(BF)

    @pl.when(odd)
    def _():
        def one(c, carry):
            r = pl.multiple_of(c * ROWS, ROWS)
            rows = pl.ds(r, ROWS)

            @pl.when(s == last)
            def _():
                own = (lax.broadcasted_iota(jnp.int32, (ROWS, 8), 1) == segc[rows, :8]).astype(BF)
                through_norm(c, split_mm(own, gpool[...]))

            @pl.when(s < last)
            def _():
                grad_prev(c).wait_recv()
                through_norm(c, G[rows, :].astype(F32))

            dx = ffn_back_rows(low[rows, :], W, V, slope, gup, r, ROWS)
            gout[rows, :] = (resid[rows, :] + dx).astype(BF)
            grad_prev(c).start()
            return carry

        lax.fori_loop(0, chunks, one, 0)
        for h in range(2):
            o_dw[h] = mm(X[...], gup[h], 0, 0).astype(BF)
            o_dv[h] = mm(act[h], low[...], 0, 0).astype(BF)
        for c in range(chunks):
            grad_prev(c).wait_send()

    @pl.when(even)
    def _():
        def one(c, carry):
            rows = pl.ds(pl.multiple_of(c * ROWS, ROWS), ROWS)
            grad_prev(c).wait_recv()
            through_norm(c, G[rows, :].astype(F32))
            return carry

        lax.fori_loop(0, chunks, one, 0)
        attn_back_core(low, W, qkv, prob, dqkv, n_qkv)

        def back(c, carry):
            rows = pl.ds(pl.multiple_of(c * ROWS, ROWS), ROWS)
            dx = mm(dqkv[0, rows, :], W[0, :, :n_qkv], 1, 1) + mm(dqkv[1, rows, :], W[1, :, :n_qkv], 1, 1)
            grad = (resid[rows, :] + dx).astype(BF)

            @pl.when(s > 0)
            def _():
                gout[rows, :] = grad
                grad_prev(c).start()

            @pl.when(s == 0)
            def _():
                width = gsplit.shape[2]
                for t in range(sections):
                    gsplit[t, rows, :] = grad[:, t * width : (t + 1) * width]

            return carry

        lax.fori_loop(0, chunks, back, 0)

        @pl.when(s == 0)
        def _():
            for t in range(sections):
                for c in range(2):
                    if t > 0:
                        spread(t, c).start()
                    else:
                        @pl.when(m != c)
                        def _():
                            spread(t, c).start()

                        @pl.when(m == c)
                        def _():
                            pltpu.make_async_copy(
                                gsplit.at[t, pl.ds(c * ROWS, ROWS)], o_gin.at[m], is_.at[t * 2 + c]
                            ).start()

        half = n_qkv // 3
        for h in range(2):
            o_dw[h, :, :n_qkv] = mm(X[...], dqkv[h], 0, 0).astype(BF)
            o_dw[h, :, n_qkv:] = mm(low[...], mixed[:, h * half : (h + 1) * half], 0, 0).astype(BF)
            o_dv[h] = jnp.zeros_like(o_dv[h])

        @pl.when(s > 0)
        def _():
            for c in range(chunks):
                grad_prev(c).wait_send()

        @pl.when(s == 0)
        def _():
            for t in range(sections):
                for c in range(2):
                    if t > 0:
                        spread(t, c).wait_send()
                    else:
                        @pl.when(m != c)
                        def _():
                            spread(t, c).wait_send()

                        @pl.when(m == c)
                        def _():
                            pltpu.make_async_copy(
                                gsplit.at[t, pl.ds(c * ROWS, ROWS)], o_gin.at[m], is_.at[t * 2 + c]
                            ).wait()

    def arrival(r):
        return pltpu.make_async_remote_copy(
            src_ref=gsplit.at[0, pl.ds(0, ROWS)], dst_ref=o_gin.at[r],
            send_sem=is_.at[0], recv_sem=ir.at[r],
            device_id={"section": 0, "mp": r}, device_id_type=MESH,
        )

    for r in range(2):
        @pl.when((s != 0) | (m != r))
        def _():
            arrival(r).wait_recv()


def unit_rows(vectors):
    return vectors * lax.rsqrt(jnp.sum(vectors * vectors, axis=-1, keepdims=True) + unit_eps)


AXES = ("section", "dp", "mp")


def crop_head(pooled, own_partners, own_segments, queue):
    sections = lax.axis_size("section")
    rows_all = lax.axis_size("dp") * lax.axis_size("mp")
    crops = own_partners.shape[0]
    width = pooled.shape[-1]
    query = pooled[0, :crops]
    pick = (own_partners[:, None] == jnp.arange(crops, dtype=jnp.int32)[None, :]).astype(F32)
    query_own = unit_rows(query).astype(BF)
    key_low = unit_rows(pooled[1, :crops]).astype(BF)
    partner_own = jnp.dot(pick, key_low.astype(F32), precision=lax.Precision.HIGHEST).astype(BF)
    pair = lax.all_gather(jnp.stack([query_own, partner_own]), AXES, axis=0, tiled=False)
    pair = pair[(sections - 1) * rows_all :]
    query_low = pair[:, 0].reshape(-1, width)
    partner_low = pair[:, 1].reshape(-1, width)
    pos_logit = jnp.sum(query_low.astype(F32) * partner_low.astype(F32), axis=-1) * inv_tau
    queue_low = unit_rows(queue.astype(F32)).astype(BF)
    neg_logit = jnp.einsum("cd,jd->cj", query_low, queue_low, preferred_element_type=F32) * inv_tau
    neg_weight = jnp.exp(neg_logit - inv_tau)
    partial_total = jnp.sum(neg_weight, axis=-1)
    partial_pull = split_right(neg_weight, queue_low)
    both = jnp.concatenate(
        [partial_pull, jnp.broadcast_to(partial_total[:, None], (partial_total.shape[0], 128))], axis=1
    )
    both = lax.psum(both, AXES)
    queue_total, queue_pull = both[:, width], both[:, :width]
    denominator = jnp.exp(pos_logit - inv_tau) + queue_total
    log_total = inv_tau + jnp.log(denominator)
    loss_value = jnp.mean(log_total - pos_logit)
    start = (lax.axis_index("dp") * lax.axis_size("mp") + lax.axis_index("mp")) * crops

    def own(value):
        return lax.dynamic_slice_in_dim(value, start, crops, 0)

    own_denominator = own(denominator)
    pos_weight = own(jnp.exp(pos_logit - inv_tau)) / own_denominator
    grad_query = (
        own(queue_pull) / own_denominator[:, None]
        + (pos_weight - 1.0)[:, None] * own(partner_low).astype(F32)
    ) * (inv_tau / query_low.shape[0])
    grad_pooled = jax.vjp(unit_rows, query)[1](grad_query)[0]
    counts = jnp.sum((own_segments[:, None] == jnp.arange(crops, dtype=jnp.int32)).astype(F32), axis=0)
    return loss_value, jnp.pad(grad_pooled / counts[:, None], ((0, 8 - crops), (0, 0)))


def split_right(weights, values):
    high = weights.astype(BF)
    rest = (weights - high.astype(F32)).astype(BF)
    return jnp.dot(high, values, preferred_element_type=F32) + jnp.dot(
        rest, values, preferred_element_type=F32
    )


def local(
    hidden_in, segments, partners, queue, first_weight, second_weight, out_bias, ln_gain, ln_bias
):
    m = lax.axis_index("mp")
    width = hidden_in.shape[-1]
    seq = segments.shape[1]
    w1 = first_weight.reshape(2, width, -1)
    w2 = second_weight.reshape(2, -1, width)
    cols = w1.shape[2]
    n_qkv = cols // 4 * 3
    heads = 2 * (cols // 4) // HD
    own_segments = lax.dynamic_index_in_dim(segments, m, 0, keepdims=False)
    own_partners = lax.dynamic_index_in_dim(partners, m, 0, keepdims=False)
    segc = jnp.broadcast_to(own_segments[:, None], (seq, 128))
    segr = jnp.broadcast_to(own_segments[None, :], (8, seq))
    small = jnp.stack([out_bias[:, 0], ln_gain[:, 0], ln_bias[:, 0]], axis=1)
    small = jnp.pad(small, ((0, 0), (0, 5), (0, 0)))
    anyspace = pl.BlockSpec(memory_space=pl.ANY)
    vmem = pl.BlockSpec(memory_space=pltpu.VMEM)
    shape = jax.ShapeDtypeStruct
    dma = pltpu.SemaphoreType.DMA
    saved = [
        shape((2, seq, n_qkv), BF), shape((heads, seq, seq), BF), shape((seq, width), BF),
        shape((2, seq, cols), BF), shape((2, seq, cols), BF), shape((seq, width), F32),
        shape((seq, 128), F32), shape((seq, width), BF), shape((2, width, cols), BF),
        shape((2, cols, width), BF),
    ]
    *kept, pooled = pl.pallas_call(
        forward_kernel,
        out_shape=saved + [shape((2, 8, width), F32)],
        in_specs=[anyspace] * 3 + [vmem] * 3,
        out_specs=[anyspace] * 10 + [vmem],
        scratch_shapes=[
            pltpu.VMEM((2, 2, width, cols), BF), pltpu.VMEM((2, 2, cols, width), BF),
            pltpu.VMEM((2, seq, width), BF), pltpu.VMEM((2, seq, width), BF),
            pltpu.VMEM((2, 2, seq, n_qkv), BF), pltpu.VMEM((heads, seq, seq), BF),
            pltpu.VMEM((2, seq, width), BF), pltpu.VMEM((2, seq, cols), BF),
            pltpu.VMEM((2, seq, cols), BF), pltpu.VMEM((seq, width), F32),
            pltpu.VMEM((seq, width), F32), pltpu.VMEM((seq, 128), F32),
            dma((6,)), dma((2,)), dma((2,)), dma((2,)), dma((2,)), dma((2,)), dma((2,)), dma((2,)), dma((2,)),
            dma((2,)), dma((2,)), dma((2, seq // ROWS)), dma((2, seq // ROWS)), dma((10,)),
        ],
        compiler_params=pltpu.CompilerParams(
            collective_id=0, has_side_effects=True, vmem_limit_bytes=VMEM_BYTES
        ),
        name="forward",
    )(hidden_in, w1, w2, segc, segr, small)
    loss_value, grad_pooled = crop_head(pooled, own_partners, own_segments, queue)
    half_width = width // lax.axis_size("section")
    gin, dw, dv, sums = pl.pallas_call(
        backward_kernel,
        out_shape=[
            shape((2, seq // 2, half_width), BF), shape((2, width, cols), BF),
            shape((2, cols, width), BF), shape((8, width), F32),
        ],
        in_specs=[anyspace] * 10 + [vmem] * 3,
        out_specs=[vmem] * 4,
        scratch_shapes=[pltpu.VMEM(a.shape, a.dtype) for a in saved]
        + [
            pltpu.VMEM((seq, width), BF), pltpu.VMEM((seq, width), BF), pltpu.VMEM((seq, width), BF),
            pltpu.VMEM((seq, width), F32), pltpu.VMEM((2, seq, cols), BF), pltpu.VMEM((2, seq, n_qkv), BF),
            pltpu.VMEM((lax.axis_size("section"), seq, half_width), BF),
            dma((10,)), dma((seq // ROWS,)), dma((seq // ROWS,)), dma((2 * lax.axis_size("section"),)), dma((2,)),
        ],
        compiler_params=pltpu.CompilerParams(
            collective_id=1, has_side_effects=True, vmem_limit_bytes=VMEM_BYTES
        ),
        name="backward",
    )(*kept, grad_pooled, segc, small[0])
    va_rows = w2.shape[1]
    returned = lax.ppermute(
        dv[:, :va_rows], "section", [(i + 1, i) for i in range(lax.axis_size("section") - 1)]
    )
    section_kind = lax.axis_index("section") % 2
    grad_second = jnp.where(section_kind == 0, returned, dv[:, va_rows:])
    flat = jnp.concatenate([dw.reshape(2, -1), grad_second.reshape(2, -1)], axis=1)
    mine = lax.psum_scatter(flat, "mp", scatter_dimension=0, tiled=False)
    total = lax.psum(mine, "dp").astype(F32)
    grad_first = total[: width * cols].reshape(width, 4, -1)
    grad_second = total[width * cols :].reshape(second_weight.shape[2:])
    sums = lax.psum(sums, ("dp", "mp"))
    return (
        loss_value, gin, grad_first[None], grad_second[None], sums[0:1], sums[1:2], sums[2:3],
    )


def solution(mesh):
    in_specs = (
        P("dp", "mp", None), P("dp", None), P("dp", None), P(("section", "dp", "mp"), None),
        P(None, "section", None, None, "mp"), P(None, "section", None, "mp", None),
        P(None, "section", None), P(None, "section", None), P(None, "section", None),
    )
    out_specs = (
        P(), P("dp", "mp", "section"), P("section", None, None, "mp"), P("section", None, "mp", None),
        P("section", None), P("section", None), P("section", None),
    )
    return jax.shard_map(local, mesh=mesh, in_specs=in_specs, out_specs=out_specs, check_vma=False)
```

time: 1760 us -> 824 us (0.47)
  waiting for transfers between devices: 904 us -> 298 us
  starting transfers between devices: 282 us -> 8.25 us
  Pallas kernels: 0 us -> 203 us
  matrix products: 116 us -> 2.29 us
  other arithmetic: 145 us -> 77.2 us
  blocking collectives: 146 us -> 98.4 us
  loops' own time: 44.1 us -> 0 us
  local copies, waits for them, and re-layouts: 85.9 us -> 112 us
    reduce_scatter x15 -> x0, waiting for transfers between devices: 461 us -> none  [the longest x5 329 us: section_backward(): lax.psum_scatter(as_sent(grad_part), 'mp', scatter_dimension=1, tiled=True)]
    ppermute x14 -> x1, starting transfers between devices: 281 us -> 8.13 us  [local(): lax.ppermute(dv[:, :va_rows], 'section', [(i + 1, i) for i in range(lax.a...]
    pallas_call x0 -> x2, Pallas kernels: none -> 203 us  [the longest x1 103 us: local(): pl.pallas_call(backward_kernel, out_shape=[shape((2, seq // 2, half_width...]
    ppermute x14 -> x1, waiting for transfers between devices: 185 us -> 39.6 us  [local(): lax.ppermute(dv[:, :va_rows], 'section', [(i + 1, i) for i in range(lax.a...]
    dot_general x32 -> x4, matrix products: 116 us -> 2.29 us  [the longest x1 0.93 us: crop_head(): jnp.dot(pick, key_low.astype(F32), precision=lax.Precision.HIGHEST)]
    concatenate x0 -> x2, other arithmetic: none -> 71.3 us  [the longest x1 70.6 us: local(): jnp.concatenate([dw.reshape(2, -1), grad_second.reshape(2, -1)], axis=1)]
    reduce_scatter x0 -> x1, local copies, waits for them, and re-layouts: none -> 65.3 us  [local(): mine = lax.psum_scatter(flat, 'mp', scatter_dimension=0, tiled=False)]
    reduce_sum x40 -> x3, other arithmetic: 46.7 us -> 0.43 us  [the longest x1 0.2 us: unit_rows(): vectors * lax.rsqrt(jnp.sum(vectors * vectors, axis=-1, keepdims=True) +...]
  transfers between devices with their start and end apart: 32 -> 4, of which waited for: 24 -> 4; matrix products, arithmetic and copies ran while one was open for 9% -> 2% of each run, Pallas kernels for 0% -> 0%
where the time goes in v1:
time: 824 us; the launch traced here: 815 us
  waiting for transfers between devices  298 us (36%)
  Pallas kernels  203 us (25%)
  local copies, waits for them, and re-layouts  112 us (14%)
  blocking collectives  98.4 us (12%)
  other arithmetic  77.2 us (9%)
  between operations  16 us (2%)
  starting transfers between devices  8.25 us (1%)
    psum x1, waiting for transfers between devices, crop_head(): both = lax.psum(both, AXES)  124 us
    pallas_call x1, Pallas kernels, local(): pl.pallas_call(backward_kernel, out_shape=[shape((2, seq // 2, half_width...  103 us
    psum x1, waiting for transfers between devices, local(): total = lax.psum(mine, 'dp').astype(F32)  102 us
    pallas_call x1, Pallas kernels, local(): pl.pallas_call(forward_kernel, out_shape=saved + [shape((2, 8, width), F3...  100 us
    concatenate x1, other arithmetic, local(): jnp.concatenate([dw.reshape(2, -1), grad_second.reshape(2, -1)], axis=1)  70.6 us
    all_gather x1, blocking collectives, crop_head(): lax.all_gather(jnp.stack([query_own, partner_own]), AXES, axis=0, tiled=F...  67.8 us
    reduce_scatter x1, local copies, waits for them, and re-layouts, local(): mine = lax.psum_scatter(flat, 'mp', scatter_dimension=0, tiled=False)  65.3 us
    ppermute x1, waiting for transfers between devices, local(): lax.ppermute(dv[:, :va_rows], 'section', [(i + 1, i) for i in range(lax.a...  39.6 us
  transfers between devices with their start and end apart: 4, of which 4 were waited for; matrix products, arithmetic and copies ran while one was open for 2% of the time, Pallas kernels for 0%

profile of v1, /device:TPU:2, one launch (start us, length us, event | category | flops | bytes accessed | tf_op | source)
XLA Modules:
  0.0 814.9 jit_solution(9728266851536367570)
XLA Ops:
  7.3 8.8 %reshape.79.w1 = bf16[2,768,1536]{2,1,0:T(8,128)(2,1)} reshape(bf16[2,1,768,4,384]{4,3,2,1,0:T(4,128)(2,1)} %param.13) | data formatting | bytes 9437184 | tf_op jit(solution)/shard_map/reshape | solution.py:632
  16.1 0.6 select_maximum_fusion.small
  16.7 0.8 broadcast_in_dim.11.segc
  18.2 100.2 %forward.1 = (bf16[2,512,1152]{2,1,0:T(8,128)(2,1)}, bf16[12,512,512]{2,1,0:T(8,128)(2,1)}, bf16[512,768]{1,0:T(8,128)(2,1)}, bf16[2,512,1536]{2,1,0:T(8,128)(2,...) custom-call(bf16[2,256,768]{2,1,0:T(8,128)(2,1)} %hid.1, ...), custom_call_target="tpu_custom_call" | custom-call | tf_op jit(solution)/shard_map/forward/pallas_call | solution.py:653
  118.4 0.9 fusion.8
  119.3 0.8 multiply_convert_fusion
  120.1 0.9 fusion.4
  121.1 67.8 %all-gather = bf16[64,6,768]{2,1,0:T(8,128)(2,1)S(1)} all-gather(bf16[2,6,768]{2,1,0:T(8,128)(2,1)S(1)} %pad_maximum_fusion.2), channel_id=2, replica_groups=mesh['section'=4,'dp'=4,'mp'=2] {'section','dp','mp'}, dimensions={0}, use_global_device_ids=true | all-gather | bytes 608256 | tf_op jit(solution)/shard_map/all_gather | solution.py:584
  190.6 0.7 pad_maximum_fusion.1
  192.3 124.0 %all-reduce.7.cloned.1.call-done = f32[48,896]{1,0:T(8,128)} async-done(((f32[48,896]{1,0:T(8,128)}), f32[48,896]{1,0:T(8,128)}) %all-reduce.7.cloned.1.call-update) | async-done | bytes 172048 | tf_op jit(solution)/shard_map/psum | solution.py:597
  316.3 0.8 slice_reduce_fusion
  317.1 0.6 fusion.18
  317.8 0.9 slice.73
  319.1 0.6 pad.9.gpool
  319.7 102.6 %backward.1 = (bf16[2,256,192]{2,1,0:T(8,128)(2,1)}, bf16[2,768,1536]{2,1,0:T(8,128)(2,1)}, bf16[2,1536,768]{2,1,0:T(8,128)(2,1)}, f32[8,768]{1,0:T(8,128)}) custom-call(bf16[2,512,1152]{2,1,0:T(8,128)(2,1)} %get-tuple-element.23.i_qkv, bf16[12,512,512]{2,1,0:T(8,128)(2,1)} %get-tuple-element.24.i_p, bf16[512,768]{1,0:T(8,128)(2,1)} %get-tuple-element.25.i_mixed, ...), custom_call_target="tpu_custom_call" | custom-call | tf_op jit(solution)/shard_map/backward/pallas_call | solution.py:675
  422.3 3.2 slice.62
  425.5 8.1 collective-permute-start
  433.7 9.4 %copy.28 = bf16[1,2,768,1536]{3,1,2,0:T(2,128)(2,1)} copy(bf16[1,2,768,1536]{3,2,1,0:T(8,128)(2,1)} %bitcast.48) | data formatting | bytes 9437184
  443.1 39.6 %collective-permute-done = bf16[2,768,768]{2,1,0:T(8,128)(2,1)S(1)} collective-permute-done((bf16[2,768,768]{2,1,0:T(8,128)(2,1)}, bf16[2,768,768]{2,1,0:T(8,128)(2,1)S(1)}, u32[]{:S(2)}, u32[]{:S(2)}) %collective-permute-start) | collective-permute-done | bytes 2359328 | tf_op jit(solution)/shard_map/ppermute | solution.py:696
  482.6 2.0 select_bitcast_fusion
  484.7 2.4 copy.29
  487.1 70.6 %pad_maximum_fusion = bf16[2,1769472]{1,0:T(2,128)(2,1)} fusion(bf16[2,589824]{1,0:T(2,128)(2,1)S(1)} %bitcast.47, bf16[2,1179648]{1,0:T(2,128)(2,1)S(1)} %bitcast.46), kind=kLoop, calls=%fused_computation | loop fusion | flops 14155776 | bytes 14155776 | tf_op jit(solution)/shard_map/concatenate | solution.py:701
  558.9 32.4 %all-reduce.11.cloned.1.call-done = bf16[2,1769472]{1,0:T(2,128)(2,1)} async-done(((bf16[2,1769472]{1,0:T(2,128)(2,1)}), bf16[2,1769472]{1,0:T(2,128)(2,1)}) %all-reduce.11.cloned.1.call-update) | async-done | bytes 7077904
  591.3 65.3 %dynamic-slice_reduce_fusion = bf16[1769472]{0:T(1024)(128)(2,1)} fusion(bf16[2,1769472]{1,0:T(2,128)(2,1)} %all-reduce.11.cloned.1.call-done, u32[]{:T(128)} %bitcast.8), kind=kLoop, calls=%fused_computation.1 | loop fusion | bytes 7077892 | tf_op jit(solution)/shard_map/reduce_scatter | solution.py:702
  656.6 0.9 copy-done.7
  657.5 0.8 copy.25
  659.0 30.7 %psum.23 = f32[8,768]{1,0:T(8,128)S(1)} all-reduce(f32[8,768]{1,0:T(8,128)S(1)} %copy-done.8), channel_id=1, replica_groups=mesh['section'=4,'dp'=4,'mp'=2] {'dp','mp'}, use_global_device_ids=true, to_apply=%region_11.12 | all-reduce | flops 6144 | bytes 49152 | tf_op jit(solution)/shard_map/psum | solution.py:706
  690.3 101.7 %all-reduce.9.cloned.1.call-done = bf16[1769472]{0:T(1024)(128)(2,1)} async-done(((bf16[1769472]{0:T(1024)(128)(2,1)}), bf16[1769472]{0:T(1024)(128)(2,1)}) %all-reduce.9.cloned.1.call-update) | async-done | bytes 3538960 | tf_op jit(solution)/shard_map/psum | solution.py:703
  791.9 3.5 slice.75
  795.5 6.6 broadcast_in_dim_reshape.4
  802.1 1.6 slice.76
  803.7 3.4 slice.66
  (58 shorter events, 5.7 us)
Async XLA Ops:
  7.2 8.9 %copy-start = (s32[2,512]{1,0:T(2,128)S(1)}, s32[2,512]{1,0:T(2,128)}, u32[]{:S(2)}) copy-start(s32[2,512]{1,0:T(2,128)} %param.10) | copy-start | bytes 12292
  7.2 309.1 %all-reduce.7.cloned.1.call-start = ((), (), s32[]{:S(2)}) async-start(), calls=%async_computation | async-start | bytes 344064 | tf_op jit(solution)/shard_map/psum | solution.py:597
  7.2 8.8 %copy-start.9 = (f32[2,1,768]{2,1,0:T(1,128)S(1)}, f32[2,1,768]{2,1,0:T(1,128)}, u32[]{:S(2)}) copy-start(f32[2,1,768]{2,1,0:T(1,128)} %param.17) | copy-start | bytes 18436
  7.2 8.8 %copy-start.10 = (f32[2,1,768]{2,1,0:T(1,128)S(1)}, f32[2,1,768]{2,1,0:T(1,128)}, u32[]{:S(2)}) copy-start(f32[2,1,768]{2,1,0:T(1,128)} %param.16) | copy-start | bytes 18436
  7.3 8.8 %copy-start.11 = (f32[2,1,768]{2,1,0:T(1,128)S(1)}, f32[2,1,768]{2,1,0:T(1,128)}, u32[]{:S(2)}) copy-start(f32[2,1,768]{2,1,0:T(1,128)} %param.15) | copy-start | bytes 18436
  18.2 101.1 %copy-start.12 = (s32[2,6]{1,0:T(2,128)S(1)}, s32[2,6]{1,0:T(2,128)}, u32[]{:S(2)}) copy-start(s32[2,6]{1,0:T(2,128)} %param.11) | copy-start | bytes 148
  18.2 170.7 %copy-start.4 = (bf16[512,768]{1,0:T(8,128)(2,1)S(1)}, bf16[512,768]{1,0:T(8,128)(2,1)}, u32[]{:S(2)}) copy-start(bf16[512,768]{1,0:T(8,128)(2,1)} %param.12) | copy-start | bytes 2359300
  120.1 71.3 %copy-start.5 = (f32[2,8,768]{2,1,0:T(8,128)S(1)}, f32[2,8,768]{2,1,0:T(8,128)}, u32[]{:S(2)}) copy-start(f32[2,8,768]{2,1,0:T(8,128)} %select_maximum_fusion.small) | copy-start | bytes 147460
  188.8 129.9 %copy-start.6 = (f32[2,8,768]{2,1,0:T(8,128)S(1)}, f32[2,8,768]{2,1,0:T(8,128)}, u32[]{:S(2)}) copy-start(f32[2,8,768]{2,1,0:T(8,128)} %get-tuple-element.22) | copy-start | bytes 147460
  191.3 400.0 %all-reduce.11.cloned.1.call-start = ((), (), s32[]{:S(2)}) async-start(), calls=%async_computation.2 | async-start | bytes 14155776
  425.5 57.1 %collective-permute-start = (bf16[2,768,768]{2,1,0:T(8,128)(2,1)}, bf16[2,768,768]{2,1,0:T(8,128)(2,1)S(1)}, u32[]{:S(2)}, u32[]{:S(2)}) collective-permute-start(bf16[2,768,768]{2,1,0:T(8,128)(2,1)} %slice.62), channel_id=1, source_target_pairs={{8,0},{16,8},{24,16},{9,1},{17,9},{25,17},{10,2},{18,10},{26,18},{... | collective-permute-start | bytes 7077896 | tf_op jit(solution)/shard_map/ppermute | solution.py:696
  484.7 2.4 copy-start.2
  557.7 0.7 copy-start.13
  557.7 234.2 %all-reduce.9.cloned.1.call-start = ((), (), s32[]{:S(2)}) async-start(), calls=%async_computation.1 | async-start | bytes 7077888 | tf_op jit(solution)/shard_map/psum | solution.py:703
  656.6 0.9 copy-start.7
  656.6 2.4 copy-start.8
  795.5 6.6 copy-start.3
  802.1 4.9 copy-start.1
Sparse Core Ops, SparseCore 0:
  191.4 124.8 all-reduce.6
  557.9 33.4 all-reduce.10
  656.7 135.1 all-reduce.8

commit v2 on v1

--- a/solution.py
+++ b/solution.py
@@ -83,29 +83,31 @@
     return act, slope
 
 
-def ffn_rows(x, w_ref, v_ref, act_ref, slope_ref, row0, rows, tile=512):
+def ffn_rows(x, w_ref, v_ref, keep_ref, row0, rows, tile=512):
     acc = None
     for h in range(2):
         n = w_ref.shape[2]
         for c in range(0, n, tile):
             up = mm(x, w_ref[h, :, c : c + tile])
-            act, slope = gelu_parts(up, slope_ref is not None)
+            act, slope = gelu_parts(up, keep_ref is not None)
             act = act.astype(BF)
-            if slope_ref is not None:
-                act_ref[h, pl.ds(row0, rows), c : c + tile] = act
-                slope_ref[h, pl.ds(row0, rows), c : c + tile] = slope.astype(BF)
+            if keep_ref is not None:
+                at = (h * n + c) // tile
+                keep_ref[at, pl.ds(row0, rows), :] = act
+                keep_ref[keep_ref.shape[0] // 2 + at, pl.ds(row0, rows), :] = slope.astype(BF)
             part = mm(act, v_ref[h, c : c + tile, :])
             acc = part if acc is None else acc + part
     return acc
 
 
-def ffn_back_rows(low, w_ref, v_ref, slope_ref, gup_ref, row0, rows, tile=512):
+def ffn_back_rows(low, w_ref, v_ref, keep_ref, gup_ref, row0, rows, tile=512):
     acc = None
     for h in range(2):
         n = w_ref.shape[2]
         for c in range(0, n, tile):
             dact = mm(low, v_ref[h, c : c + tile, :], 1, 1)
-            gup = (dact * slope_ref[h, pl.ds(row0, rows), c : c + tile].astype(F32)).astype(BF)
+            at = keep_ref.shape[0] // 2 + (h * n + c) // tile
+            gup = (dact * keep_ref[at, pl.ds(row0, rows), :].astype(F32)).astype(BF)
             gup_ref[h, pl.ds(row0, rows), c : c + tile] = gup
             part = mm(gup, w_ref[h, :, c : c + tile], 1, 1)
             acc = part if acc is None else acc + part
@@ -162,8 +164,8 @@
 
 def forward_kernel(
     hid, w1, w2, segc, segr, small,
-    o_qkv, o_p, o_mixed, o_act, o_slope, o_xhat, o_rstd, o_x, o_w, o_v, o_pool,
-    W, V, X, Y, qkv, prob, mixed, act, slope, yf, xhat, rstd,
+    o_qkv, o_p, o_mixed, o_xhat, o_rstd, o_x, o_w, o_v, o_pool,
+    W, V, X, Y, qkv, prob, mixed, yf, xhat, rstd,
     l_sem, ws, wr, vbs, vbr, vas, var, vfs, vfr, hs, hr, acs, acr, o_sem,
 ):
     s, m = lax.axis_index("section"), lax.axis_index("mp")
@@ -266,7 +268,7 @@
 
     def saves(e):
         pairs = [
-            (qkv.at[0], o_qkv), (prob, o_p), (mixed.at[0], o_mixed), (act, o_act), (slope, o_slope),
+            (qkv.at[0], o_qkv), (prob, o_p), (mixed.at[0], o_mixed),
             (xhat, o_xhat), (rstd, o_rstd), (X.at[0], o_x), (W.at[0], o_w), (V.at[0], o_v),
         ]
         return [pltpu.make_async_copy(a, b, o_sem.at[i]) for i, (a, b) in enumerate(pairs)]
@@ -321,10 +323,7 @@
             r = pl.multiple_of(c * ROWS, ROWS)
             rows = pl.ds(r, ROWS)
             x = X[e, rows, :]
-            if e == 0:
-                branch = ffn_rows(x, W.at[e], V.at[e], act, slope, r, ROWS)
-            else:
-                branch = ffn_rows(x, W.at[e], V.at[e], None, None, r, ROWS)
+            branch = ffn_rows(x, W.at[e], V.at[e], prob if e == 0 else None, r, ROWS)
             y = finish(e, rows, x.astype(F32) + branch + small[e, 0:1, :])
 
             @pl.when(s < last)
@@ -385,25 +384,33 @@
                 act_next(e, c).wait_send()
 
 
+PIECES = 16
+WAIT_ROOT = 2
+LAG = 3
+
+
 def backward_kernel(
-    i_qkv, i_p, i_mixed, i_act, i_slope, i_xhat, i_rstd, i_x, i_w, i_v, gpool, segc, small,
-    o_gin, o_dw, o_dv, o_sum,
-    qkv, prob, mixed, act, slope, xhat, rstd, X, W, V, G, gout, low, resid, gup, dqkv, gsplit,
-    i_sem, gs, gr, is_, ir,
+    i_qkv, i_p, i_mixed, i_xhat, i_rstd, i_x, i_w, i_v, gpool, segc, small,
+    o_gin, o_red, o_sum,
+    qkv, prob, mixed, xhat, rstd, X, W, V, G, gout, low, resid, gup, gsplit,
+    mine, give, taken, part, sums,
+    i_sem, gs, gr, is_, ir, xs, xr, ps, pr, fs, fr, vs, vr, ss, sr,
 ):
-    s, m = lax.axis_index("section"), lax.axis_index("mp")
-    sections = lax.axis_size("section")
+    s, d, m = lax.axis_index("section"), lax.axis_index("dp"), lax.axis_index("mp")
+    sections, planes = lax.axis_size("section"), lax.axis_size("dp")
     last = sections - 1
-    seq = X.shape[0]
+    other = 1 - m
+    seq, width = X.shape
     chunks = seq // ROWS
     n_qkv = qkv.shape[2]
+    cols = W.shape[2]
     even = lax.rem(s, 2) == 0
     odd = lax.rem(s, 2) == 1
     loads = [
         pltpu.make_async_copy(a, b, i_sem.at[i])
         for i, (a, b) in enumerate(
-            [(i_qkv, qkv), (i_p, prob), (i_mixed, mixed), (i_act, act), (i_slope, slope),
-             (i_xhat, xhat), (i_rstd, rstd), (i_x, X), (i_w, W), (i_v, V)]
+            [(i_xhat, xhat), (i_rstd, rstd), (i_v, V), (i_p, prob), (i_w, W), (i_x, X),
+             (i_qkv, qkv), (i_mixed, mixed)]
         )
     ]
     for copy in loads:
@@ -416,36 +423,64 @@
             def _():
                 pl.semaphore_signal(barrier, inc=1, device_id={"section": t, "mp": c}, device_id_type=MESH)
 
-    pl.semaphore_wait(barrier, 2 * sections - 1)
+    def greet(i, carry):
+        to = lax.rem(d + 1 + i, planes)
+        for c in range(2):
+            pl.semaphore_signal(barrier, inc=1, device_id={"dp": to, "mp": c}, device_id_type=MESH)
+        return carry
+
+    lax.fori_loop(0, planes - 1, greet, 0)
+    pl.semaphore_wait(barrier, 2 * sections - 1 + 2 * (planes - 1))
+
+    def remote(src, dst, send, recv, **to):
+        return pltpu.make_async_remote_copy(
+            src_ref=src, dst_ref=dst, send_sem=send, recv_sem=recv, device_id=to, device_id_type=MESH
+        )
 
     def grad_prev(c):
         rows = pl.ds(pl.multiple_of(c * ROWS, ROWS), ROWS)
-        return pltpu.make_async_remote_copy(
-            src_ref=gout.at[rows], dst_ref=G.at[rows], send_sem=gs.at[c], recv_sem=gr.at[c],
-            device_id={"section": s - 1}, device_id_type=MESH,
-        )
+        return remote(gout.at[rows], G.at[rows], gs.at[c], gr.at[c], section=s - 1)
 
     def spread(t, c):
-        return pltpu.make_async_remote_copy(
-            src_ref=gsplit.at[t, pl.ds(c * ROWS, ROWS)], dst_ref=o_gin.at[m],
-            send_sem=is_.at[t * 2 + c], recv_sem=ir.at[m],
-            device_id={"section": t, "mp": c}, device_id_type=MESH,
+        return remote(
+            gsplit.at[t, pl.ds(c * ROWS, ROWS)], o_gin.at[m], is_.at[t * 2 + c], ir.at[m], section=t, mp=c
         )
 
     for copy in loads:
         copy.wait()
 
-    o_sum[...] = jnp.zeros_like(o_sum)
+    own_slot = d * 2 + m
+    sums[own_slot] = jnp.zeros_like(sums[own_slot])
 
     def through_norm(c, g):
         rows = pl.ds(pl.multiple_of(c * ROWS, ROWS), ROWS)
         xh = xhat[rows, :]
         grad = norm_back(g, xh, rstd[rows, :1], small[1:2, :])
-        o_sum[0:1, :] += jnp.sum(grad, axis=0, keepdims=True)
-        o_sum[1:2, :] += jnp.sum(g * xh, axis=0, keepdims=True)
-        o_sum[2:3, :] += jnp.sum(g, axis=0, keepdims=True)
+        sums[own_slot, 0:1, :] += jnp.sum(grad, axis=0, keepdims=True)
+        sums[own_slot, 1:2, :] += jnp.sum(g * xh, axis=0, keepdims=True)
+        sums[own_slot, 2:3, :] += jnp.sum(g, axis=0, keepdims=True)
         resid[rows, :] = grad
         low[rows, :] = grad.astype(BF)
+
+    def exchange(kind):
+        return remote(give.at[kind], taken.at[kind], xs.at[kind], xr.at[kind], mp=other)
+
+    def sum_to(i):
+        to = lax.rem(own_slot + 1 + i, 2 * planes)
+        return remote(
+            sums.at[own_slot], sums.at[own_slot], ss.at[i], sr.at[own_slot], dp=to // 2, mp=lax.rem(to, 2)
+        )
+
+    def sum_from(i):
+        slot = lax.rem(own_slot + 1 + i, 2 * planes)
+        return remote(sums.at[slot], sums.at[slot], ss.at[i], sr.at[slot], dp=slot // 2, mp=lax.rem(slot, 2))
+
+    def start_sums():
+        def one(i, carry):
+            sum_to(i).start()
+            return carry
+
+        lax.fori_loop(0, 2 * planes - 1, one, 0)
 
     @pl.when(odd)
     def _():
@@ -463,17 +498,27 @@
                 grad_prev(c).wait_recv()
                 through_norm(c, G[rows, :].astype(F32))
 
-            dx = ffn_back_rows(low[rows, :], W, V, slope, gup, r, ROWS)
+            dx = ffn_back_rows(low[rows, :], W, V, prob, gup, r, ROWS)
             gout[rows, :] = (resid[rows, :] + dx).astype(BF)
             grad_prev(c).start()
             return carry
 
         lax.fori_loop(0, chunks, one, 0)
-        for h in range(2):
-            o_dw[h] = mm(X[...], gup[h], 0, 0).astype(BF)
-            o_dv[h] = mm(act[h], low[...], 0, 0).astype(BF)
-        for c in range(chunks):
-            grad_prev(c).wait_send()
+        start_sums()
+        unit = 256
+        for h, out in ((other, give), (m, mine)):
+            for c in range(cols // unit):
+                act = prob[h * (cols // 512) + c * unit // 512, :, c * unit % 512 : c * unit % 512 + unit]
+                r, q = c * unit % width, c * unit // width * width
+                out[0, r : r + unit, q : q + width] = mm(act, low[...], 0, 0).astype(BF)
+            if out is give:
+                exchange(0).start()
+        for h, out in ((other, give), (m, mine)):
+            for c in range(0, cols, 512):
+                out[1, :, c : c + 512] = mm(X[...], gup[h, :, c : c + 512], 0, 0).astype(BF)
+            if out is give:
+                exchange(1).start()
+        exchange(0).wait_recv()
 
     @pl.when(even)
     def _():
@@ -484,11 +529,14 @@
             return carry
 
         lax.fori_loop(0, chunks, one, 0)
-        attn_back_core(low, W, qkv, prob, dqkv, n_qkv)
+        start_sums()
+        attn_back_core(low, W, qkv, prob, gup, n_qkv)
 
         def back(c, carry):
             rows = pl.ds(pl.multiple_of(c * ROWS, ROWS), ROWS)
-            dx = mm(dqkv[0, rows, :], W[0, :, :n_qkv], 1, 1) + mm(dqkv[1, rows, :], W[1, :, :n_qkv], 1, 1)
+            dx = mm(gup[0, rows, :n_qkv], W[0, :, :n_qkv], 1, 1) + mm(
+                gup[1, rows, :n_qkv], W[1, :, :n_qkv], 1, 1
+            )
             grad = (resid[rows, :] + dx).astype(BF)
 
             @pl.when(s > 0)
@@ -498,9 +546,9 @@
 
             @pl.when(s == 0)
             def _():
-                width = gsplit.shape[2]
+                part_width = gsplit.shape[2]
                 for t in range(sections):
-                    gsplit[t, rows, :] = grad[:, t * width : (t + 1) * width]
+                    gsplit[t, rows, :] = grad[:, t * part_width : (t + 1) * part_width]
 
             return carry
 
@@ -524,44 +572,196 @@
                             ).start()
 
         half = n_qkv // 3
-        for h in range(2):
-            o_dw[h, :, :n_qkv] = mm(X[...], dqkv[h], 0, 0).astype(BF)
-            o_dw[h, :, n_qkv:] = mm(low[...], mixed[:, h * half : (h + 1) * half], 0, 0).astype(BF)
-            o_dv[h] = jnp.zeros_like(o_dv[h])
-
-        @pl.when(s > 0)
-        def _():
-            for c in range(chunks):
-                grad_prev(c).wait_send()
-
-        @pl.when(s == 0)
-        def _():
-            for t in range(sections):
-                for c in range(2):
-                    if t > 0:
+        for h, out in ((other, give), (m, mine)):
+            for c in range(0, n_qkv, half):
+                out[1, :, c : c + half] = mm(X[...], gup[h, :, c : c + half], 0, 0).astype(BF)
+            for k in range(2):
+                @pl.when(h == k)
+                def _():
+                    out[1, :, n_qkv:] = mm(low[...], mixed[:, k * half : (k + 1) * half], 0, 0).astype(BF)
+            if out is give:
+                exchange(1).start()
+
+    exchange(1).wait_recv()
+
+    step_rows = width // PIECES
+    root_a, root_b = (planes - 1) // 2, planes // 2
+    first = jnp.where(odd, 0, PIECES)
+    total = 2 * PIECES
+    lag = WAIT_ROOT + LAG * jnp.maximum(root_b - d, d - root_a)
+
+    def place(i):
+        kind = i // PIECES
+        rows = pl.ds(pl.multiple_of(lax.rem(i, PIECES) * step_rows, step_rows), step_rows)
+        root = jnp.where(lax.rem(i, 2) == 0, root_a, root_b)
+        return kind, rows, root
+
+    def part_right(i):
+        kind, rows, _ = place(i)
+        return remote(mine.at[kind, rows], part.at[0, kind, rows], ps.at[i], pr.at[0, i], dp=d + 1)
+
+    def part_left(i):
+        kind, rows, _ = place(i)
+        return remote(mine.at[kind, rows], part.at[1, kind, rows], ps.at[i], pr.at[1, i], dp=d - 1)
+
+    def whole(i, side, src):
+        kind, rows, _ = place(i)
+        return remote(src.at[kind, rows], o_red.at[kind, rows], fs.at[side, i], fr.at[i], dp=d + (1 if side else -1))
+
+    def keep_root(i):
+        kind, rows, _ = place(i)
+        return pltpu.make_async_copy(mine.at[kind, rows], o_red.at[kind, rows], fr.at[i])
+
+    def down_prev(i):
+        _, rows, _ = place(i)
+        return remote(
+            o_red.at[0, rows, pl.ds(0, width)], o_red.at[0, rows, pl.ds(width, width)],
+            vs.at[i], vr.at[i], section=s - 1,
+        )
+
+    def add(i, *sides):
+        kind, rows, _ = place(i)
+        value = mine[kind, rows, :].astype(F32) + taken[kind, rows, :].astype(F32)
+        for side in sides:
+            value = value + part[side, kind, rows, :].astype(F32)
+        mine[kind, rows, :] = value.astype(BF)
+
+    def pieces(i, carry):
+        root = place(i)[2]
+
+        @pl.when((i < total) & (d < root))
+        def _():
+            @pl.when(d > 0)
+            def _():
+                part_right(i).wait_recv()
+                add(i, 0)
+
+            @pl.when(d == 0)
+            def _():
+                add(i)
+
+            part_right(i).start()
+
+        @pl.when((i < total) & (d > root))
+        def _():
+            @pl.when(d < planes - 1)
+            def _():
+                part_left(i).wait_recv()
+                add(i, 1)
+
+            @pl.when(d == planes - 1)
+            def _():
+                add(i)
+
+            part_left(i).start()
+
+        k = i - WAIT_ROOT
+
+        @pl.when((k >= first) & (k < total) & (d == place(k)[2]))
+        def _():
+            part_right(k).wait_recv()
+            part_left(k).wait_recv()
+            add(k, 0, 1)
+            keep_root(k).start()
+            whole(k, 0, mine).start()
+            whole(k, 1, mine).start()
+
+        @pl.when(i >= first + lag)
+        def _():
+            j = i - lag
+            kind, _, root = place(j)
+            keep_root(j).wait()
+
+            @pl.when((d < root) & (d > 0))
+            def _():
+                whole(j, 0, o_red).start()
+
+            @pl.when((d > root) & (d < planes - 1))
+            def _():
+                whole(j, 1, o_red).start()
+
+            @pl.when(kind == 0)
+            def _():
+                down_prev(j).start()
+
+        return carry
+
+    lax.fori_loop(first, total + lag, pieces, 0)
+
+    def settle(i, carry):
+        kind, rows, root = place(i)
+
+        @pl.when(d != root)
+        def _():
+            part_right(i).wait_send()
+
+        @pl.when((d <= root) & (d > 0))
+        def _():
+            whole(i, 0, mine).wait_send()
+
+        @pl.when((d >= root) & (d < planes - 1))
+        def _():
+            whole(i, 1, mine).wait_send()
+
+        @pl.when(kind == 0)
+        def _():
+            down_prev(i).wait_send()
+
+        return carry
+
+    lax.fori_loop(first, total, settle, 0)
+
+    @pl.when(even)
+    def _():
+        def arrive(i, carry):
+            down_prev(i).wait_recv()
+            return carry
+
+        lax.fori_loop(0, PIECES, arrive, 0)
+
+    @pl.when(odd)
+    def _():
+        exchange(0).wait_send()
+
+    exchange(1).wait_send()
+
+    @pl.when(s > 0)
+    def _():
+        for c in range(chunks):
+            grad_prev(c).wait_send()
+
+    @pl.when(s == 0)
+    def _():
+        for t in range(sections):
+            for c in range(2):
+                if t > 0:
+                    spread(t, c).wait_send()
+                else:
+                    @pl.when(m != c)
+                    def _():
                         spread(t, c).wait_send()
-                    else:
-                        @pl.when(m != c)
-                        def _():
-                            spread(t, c).wait_send()
-
-                        @pl.when(m == c)
-                        def _():
-                            pltpu.make_async_copy(
-                                gsplit.at[t, pl.ds(c * ROWS, ROWS)], o_gin.at[m], is_.at[t * 2 + c]
-                            ).wait()
+
+                    @pl.when(m == c)
+                    def _():
+                        pltpu.make_async_copy(
+                            gsplit.at[t, pl.ds(c * ROWS, ROWS)], o_gin.at[m], is_.at[t * 2 + c]
+                        ).wait()
 
     def arrival(r):
-        return pltpu.make_async_remote_copy(
-            src_ref=gsplit.at[0, pl.ds(0, ROWS)], dst_ref=o_gin.at[r],
-            send_sem=is_.at[0], recv_sem=ir.at[r],
-            device_id={"section": 0, "mp": r}, device_id_type=MESH,
-        )
+        return remote(gsplit.at[0, pl.ds(0, ROWS)], o_gin.at[r], is_.at[0], ir.at[r], section=0, mp=r)
 
     for r in range(2):
         @pl.when((s != 0) | (m != r))
         def _():
             arrival(r).wait_recv()
+
+    def sums_in(i, carry):
+        sum_from(i).wait_recv()
+        sum_to(i).wait_send()
+        return carry
+
+    lax.fori_loop(0, 2 * planes - 1, sums_in, 0)
+    o_sum[...] = jnp.sum(sums[...], axis=0)
 
 
 def unit_rows(vectors):
@@ -646,24 +846,22 @@
     dma = pltpu.SemaphoreType.DMA
     saved = [
         shape((2, seq, n_qkv), BF), shape((heads, seq, seq), BF), shape((seq, width), BF),
-        shape((2, seq, cols), BF), shape((2, seq, cols), BF), shape((seq, width), F32),
-        shape((seq, 128), F32), shape((seq, width), BF), shape((2, width, cols), BF),
+        shape((seq, width), F32), shape((seq, 128), F32), shape((seq, width), BF), shape((2, width, cols), BF),
         shape((2, cols, width), BF),
     ]
     *kept, pooled = pl.pallas_call(
         forward_kernel,
         out_shape=saved + [shape((2, 8, width), F32)],
         in_specs=[anyspace] * 3 + [vmem] * 3,
-        out_specs=[anyspace] * 10 + [vmem],
+        out_specs=[anyspace] * 8 + [vmem],
         scratch_shapes=[
             pltpu.VMEM((2, 2, width, cols), BF), pltpu.VMEM((2, 2, cols, width), BF),
             pltpu.VMEM((2, seq, width), BF), pltpu.VMEM((2, seq, width), BF),
             pltpu.VMEM((2, 2, seq, n_qkv), BF), pltpu.VMEM((heads, seq, seq), BF),
-            pltpu.VMEM((2, seq, width), BF), pltpu.VMEM((2, seq, cols), BF),
-            pltpu.VMEM((2, seq, cols), BF), pltpu.VMEM((seq, width), F32),
+            pltpu.VMEM((2, seq, width), BF), pltpu.VMEM((seq, width), F32),
             pltpu.VMEM((seq, width), F32), pltpu.VMEM((seq, 128), F32),
             dma((6,)), dma((2,)), dma((2,)), dma((2,)), dma((2,)), dma((2,)), dma((2,)), dma((2,)), dma((2,)),
-            dma((2,)), dma((2,)), dma((2, seq // ROWS)), dma((2, seq // ROWS)), dma((10,)),
+            dma((2,)), dma((2,)), dma((2, seq // ROWS)), dma((2, seq // ROWS)), dma((8,)),
         ],
         compiler_params=pltpu.CompilerParams(
             collective_id=0, has_side_effects=True, vmem_limit_bytes=VMEM_BYTES
@@ -672,38 +870,33 @@
     )(hidden_in, w1, w2, segc, segr, small)
     loss_value, grad_pooled = crop_head(pooled, own_partners, own_segments, queue)
     half_width = width // lax.axis_size("section")
-    gin, dw, dv, sums = pl.pallas_call(
+    sections, planes = lax.axis_size("section"), lax.axis_size("dp")
+    gin, red, sums = pl.pallas_call(
         backward_kernel,
         out_shape=[
-            shape((2, seq // 2, half_width), BF), shape((2, width, cols), BF),
-            shape((2, cols, width), BF), shape((8, width), F32),
+            shape((2, seq // 2, half_width), BF), shape((2, width, cols), BF), shape((8, width), F32),
         ],
-        in_specs=[anyspace] * 10 + [vmem] * 3,
-        out_specs=[vmem] * 4,
+        in_specs=[anyspace] * 8 + [vmem] * 3,
+        out_specs=[vmem, anyspace, vmem],
         scratch_shapes=[pltpu.VMEM(a.shape, a.dtype) for a in saved]
         + [
             pltpu.VMEM((seq, width), BF), pltpu.VMEM((seq, width), BF), pltpu.VMEM((seq, width), BF),
-            pltpu.VMEM((seq, width), F32), pltpu.VMEM((2, seq, cols), BF), pltpu.VMEM((2, seq, n_qkv), BF),
-            pltpu.VMEM((lax.axis_size("section"), seq, half_width), BF),
-            dma((10,)), dma((seq // ROWS,)), dma((seq // ROWS,)), dma((2 * lax.axis_size("section"),)), dma((2,)),
+            pltpu.VMEM((seq, width), F32), pltpu.VMEM((2, seq, cols), BF),
+            pltpu.VMEM((sections, seq, half_width), BF),
+            pltpu.VMEM((2, width, cols), BF), pltpu.VMEM((2, width, cols), BF),
+            pltpu.VMEM((2, width, cols), BF), pltpu.VMEM((2, 2, width, cols), BF),
+            pltpu.VMEM((2 * planes, 8, width), F32),
+            dma((8,)), dma((seq // ROWS,)), dma((seq // ROWS,)), dma((2 * sections,)), dma((2,)),
+            dma((2,)), dma((2,)), dma((2 * PIECES,)), dma((2, 2 * PIECES)), dma((2, 2 * PIECES)),
+            dma((2 * PIECES,)), dma((PIECES,)), dma((PIECES,)), dma((2 * planes,)), dma((2 * planes,)),
         ],
         compiler_params=pltpu.CompilerParams(
             collective_id=1, has_side_effects=True, vmem_limit_bytes=VMEM_BYTES
         ),
         name="backward",
     )(*kept, grad_pooled, segc, small[0])
-    va_rows = w2.shape[1]
-    returned = lax.ppermute(
-        dv[:, :va_rows], "section", [(i + 1, i) for i in range(lax.axis_size("section") - 1)]
-    )
-    section_kind = lax.axis_index("section") % 2
-    grad_second = jnp.where(section_kind == 0, returned, dv[:, va_rows:])
-    flat = jnp.concatenate([dw.reshape(2, -1), grad_second.reshape(2, -1)], axis=1)
-    mine = lax.psum_scatter(flat, "mp", scatter_dimension=0, tiled=False)
-    total = lax.psum(mine, "dp").astype(F32)
-    grad_first = total[: width * cols].reshape(width, 4, -1)
-    grad_second = total[width * cols :].reshape(second_weight.shape[2:])
-    sums = lax.psum(sums, ("dp", "mp"))
+    grad_first = red[1].astype(F32).reshape(width, 4, -1)
+    grad_second = red[0, :, width:].astype(F32).reshape(second_weight.shape[2:])
     return (
         loss_value, gin, grad_first[None], grad_second[None], sums[0:1], sums[1:2], sums[2:3],
     )

time: 824 us -> 553 us (0.67)
  waiting for transfers between devices: 298 us -> 124 us
  Pallas kernels: 203 us -> 299 us
  local copies, waits for them, and re-layouts: 112 us -> 23.9 us
  other arithmetic: 77.2 us -> 11.7 us
  blocking collectives: 98.4 us -> 67.7 us
    psum x1 -> x0, waiting for transfers between devices: 102 us -> none  [local(): total = lax.psum(mine, 'dp').astype(F32)]
    pallas_call x1, Pallas kernels: 103 us -> 199 us  [local(): pl.pallas_call(backward_kernel, out_shape=[shape((2, seq // 2, half_width...]
    concatenate x1 -> x0, other arithmetic: 70.6 us -> none  [local(): jnp.concatenate([dw.reshape(2, -1), grad_second.reshape(2, -1)], axis=1)]
    reduce_scatter x1 -> x0, local copies, waits for them, and re-layouts: 65.3 us -> none  [local(): mine = lax.psum_scatter(flat, 'mp', scatter_dimension=0, tiled=False)]
    ppermute x1 -> x0, waiting for transfers between devices: 39.6 us -> none  [local(): lax.ppermute(dv[:, :va_rows], 'section', [(i + 1, i) for i in range(lax.a...]
    unnamed x4 -> x1, waiting for transfers between devices: 32.4 us -> 0.02 us
    psum x1 -> x0, blocking collectives: 30.7 us -> none  [local(): sums = lax.psum(sums, ('dp', 'mp'))]
    unnamed x33 -> x18, local copies, waits for them, and re-layouts: 14.8 us -> 0.87 us
  transfers between devices with their start and end apart: 4 -> 1, of which waited for: 4 -> 1; matrix products, arithmetic and copies ran while one was open for 2% -> 0% of each run, Pallas kernels for 0% -> 0%
where the time goes in v2:
time: 553 us; the launch traced here: 545 us
  Pallas kernels  299 us (54%)
  waiting for transfers between devices  124 us (22%)
  blocking collectives  67.7 us (12%)
  local copies, waits for them, and re-layouts  23.9 us (4%)
  between operations  16.5 us (3%)
  other arithmetic  11.7 us (2%)
    pallas_call x1, Pallas kernels, local(): pl.pallas_call(backward_kernel, out_shape=[shape((2, seq // 2, half_width...  199 us
    psum x1, waiting for transfers between devices, crop_head(): both = lax.psum(both, AXES)  124 us
    pallas_call x1, Pallas kernels, local(): pl.pallas_call(forward_kernel, out_shape=saved + [shape((2, 8, width), F3...  100 us
    all_gather x1, blocking collectives, crop_head(): lax.all_gather(jnp.stack([query_own, partner_own]), AXES, axis=0, tiled=F...  67.7 us
  transfers between devices with their start and end apart: 1, of which 1 were waited for; matrix products, arithmetic and copies ran while one was open for 0% of the time, Pallas kernels for 0%

profile of v2, /device:TPU:2, one launch (start us, length us, event | category | flops | bytes accessed | tf_op | source)
XLA Modules:
  0.0 545.3 jit_solution(17884647995075619429)
XLA Ops:
  7.2 0.7 fusion.16
  7.9 1.4 fusion
  9.3 8.8 %reshape.89.w1 = bf16[2,768,1536]{2,1,0:T(8,128)(2,1)} reshape(bf16[2,1,768,4,384]{4,3,2,1,0:T(4,128)(2,1)} %param.13) | data formatting | bytes 9437184 | tf_op jit(solution)/shard_map/reshape | solution.py:832
  18.1 0.6 select_maximum_fusion.small
  18.8 0.6 broadcast_in_dim.12.segr
  19.4 0.8 broadcast_in_dim.11.segc
  20.2 100.2 %forward.1 = (bf16[2,512,1152]{2,1,0:T(8,128)(2,1)}, bf16[12,512,512]{2,1,0:T(8,128)(2,1)}, bf16[512,768]{1,0:T(8,128)(2,1)}, f32[512,768]{1,0:T(8,128)}, f32[51...) custom-call(bf16[2,256,768]{2,1,0:T(8,128)(2,1)} %hid.1, ...), custom_call_target="tpu_custom_call" | custom-call | tf_op jit(solution)/shard_map/forward/pallas_call | solution.py:852
  120.4 0.9 fusion.8
  121.3 0.8 multiply_convert_fusion
  122.1 0.9 fusion.4
  123.1 67.7 %all-gather = bf16[64,6,768]{2,1,0:T(8,128)(2,1)S(1)} all-gather(bf16[2,6,768]{2,1,0:T(8,128)(2,1)S(1)} %pad_maximum_fusion.1), channel_id=2, replica_groups=mesh['section'=4,'dp'=4,'mp'=2] {'section','dp','mp'}, dimensions={0}, use_global_device_ids=true | all-gather | bytes 608256 | tf_op jit(solution)/shard_map/all_gather | solution.py:784
  190.9 0.6 fusion.24
  191.5 0.4 fusion.11
  191.9 0.4 convolution_add_fusion
  192.3 0.7 pad_maximum_fusion
  193.1 0.6 slice_bitcast_fusion.2.small
  193.7 0.1 multiply_reduce_fusion
  193.9 0.1 convert_reduce_fusion
  194.0 124.0 %all-reduce.4.cloned.1.call-done = f32[48,896]{1,0:T(8,128)} async-done(((f32[48,896]{1,0:T(8,128)}), f32[48,896]{1,0:T(8,128)}) %all-reduce.4.cloned.1.call-update) | async-done | bytes 172048 | tf_op jit(solution)/shard_map/psum | solution.py:797
  318.0 0.8 slice_reduce_fusion
  318.9 0.6 fusion.18
  319.6 0.9 slice.54
  320.5 0.2 fusion.9
  320.7 0.1 fusion.5
  320.8 0.6 pad.9.gpool
  321.4 198.8 %backward.1 = (bf16[2,256,192]{2,1,0:T(8,128)(2,1)}, bf16[2,768,1536]{2,1,0:T(8,128)(2,1)}, f32[8,768]{1,0:T(8,128)}) custom-call(bf16[2,512,1152]{2,1,0:T(8,128)(2,1)} %get-tuple-element.20.i_qkv, bf16[12,512,512]{2,1,0:T(8,128)(2,1)} %get-tuple-element.21.i_p, bf16[512,768]{1,0:T(8,128)(2,1)} %get-tuple-element.22.i_mixed, ...), custom_call_target="tpu_custom_call" | custom-call | tf_op jit(solution)/shard_map/backward/pallas_call | solution.py:874
  520.3 1.3 slice.47
  521.7 4.5 slice_convert_fusion
  526.1 0.8 copy.25
  527.0 1.4 fusion.22
  528.4 6.2 %reshape.91 = f32[1,768,4,384]{3,2,1,0:T(4,128)} reshape(f32[1,768,1536]{2,1,0:T(8,128)} %slice_convert_fusion) | data formatting | bytes 9437184 | tf_op jit(solution)/shard_map/convert_element_type | solution.py:898
  534.6 1.6 convert.2
  (30 shorter events, 0.4 us)
Async XLA Ops:
  7.2 0.8 copy-start
  7.2 310.9 %all-reduce.4.cloned.1.call-start = ((), (), s32[]{:S(2)}) async-start(), calls=%async_computation | async-start | bytes 344064 | tf_op jit(solution)/shard_map/psum | solution.py:797
  9.3 8.8 %copy-start.5 = (f32[2,1,768]{2,1,0:T(1,128)S(1)}, f32[2,1,768]{2,1,0:T(1,128)}, u32[]{:S(2)}) copy-start(f32[2,1,768]{2,1,0:T(1,128)} %param.17) | copy-start | bytes 18436
  9.3 8.8 %copy-start.6 = (f32[2,1,768]{2,1,0:T(1,128)S(1)}, f32[2,1,768]{2,1,0:T(1,128)}, u32[]{:S(2)}) copy-start(f32[2,1,768]{2,1,0:T(1,128)} %param.16) | copy-start | bytes 18436
  9.3 8.8 %copy-start.7 = (f32[2,1,768]{2,1,0:T(1,128)S(1)}, f32[2,1,768]{2,1,0:T(1,128)}, u32[]{:S(2)}) copy-start(f32[2,1,768]{2,1,0:T(1,128)} %param.15) | copy-start | bytes 18436
  20.2 170.7 %copy-start.1 = (bf16[512,768]{1,0:T(8,128)(2,1)S(1)}, bf16[512,768]{1,0:T(8,128)(2,1)}, u32[]{:S(2)}) copy-start(bf16[512,768]{1,0:T(8,128)(2,1)} %param.12) | copy-start | bytes 2359300
  190.8 2.2 copy-start.2
  190.8 129.7 %copy-start.3 = (f32[2,8,768]{2,1,0:T(8,128)S(1)}, f32[2,8,768]{2,1,0:T(8,128)}, u32[]{:S(2)}) copy-start(f32[2,8,768]{2,1,0:T(8,128)} %get-tuple-element.19) | copy-start | bytes 147460
  521.7 4.5 copy-start.4
Sparse Core Ops, SparseCore 0:
  193.2 124.8 all-reduce.3
